TPU v7x, 512 devices: a whole 4x4x16 slice. The times are simulated.
512 devices in a mesh: grp: 16 (over z), seq: 32 (over x, y, core).
Axes of the slice: x: 4, y: 4, z: 16, core: 2. Of those that a mesh axis runs over, the one named last changes fastest.
Arguments:
- queries: bfloat16 [1024, 4096], P('grp', 'seq'), may hold values from -30 to 30
- row_prompt: int32 [1024, 1], P('grp'), may hold values from 0 to 15; in each aligned block of 64 rows (0 to 63, 64 to 127, ...) at most 8 rows name the same one
- prompt_prefix_keys: bfloat16 [16, 32768, 512], P('grp', 'seq'), may hold values from -30 to 30
- prompt_prefix_values: bfloat16 [16, 32768, 512], P('grp', 'seq'), may hold values from -6 to 6
- row_suffix_keys: bfloat16 [1024, 128, 512], P(('grp', 'seq')), may hold values from -12 to 12
- row_suffix_values: bfloat16 [1024, 128, 512], P(('grp', 'seq')), may hold values from -6 to 6
- suffix_lengths: int32 [1024], P(('grp', 'seq')), may hold values from 1 to 128, as said below
- w_out: bfloat16 [4096, 8192], P('seq'), may hold values from -0.75 to 0.75
Outputs:
- mixed: bfloat16 [1024, 8192], P('grp', 'seq')
Inputs may be any that keep to these rules, and one draw needn't show every extreme that they name: `row_prompt`: among the 64 rows of one group no prompt is named by more than 8 rows, and some prompt reaches 8 in some groups; every prompt is named by some row. `suffix_lengths`: every draw holds a row with 128 live positions.
All inputs are finite; a program needn't handle non-finite values.
Results may differ from a plain program's by a relative error of at most 0.022.
Values may be sent and summed in bfloat16 or wider, within the bound.
No kernel may reach another device: no remote copies, remote signals or barrier semaphores. Data moves between devices by JAX's collectives and lax.ppermute only.
A program may use at most 128 MiB of HBM per device.

v0:
```python
import math

import jax
import jax.numpy as jnp
from jax import lax
from jax.sharding import PartitionSpec as P

QUERY_HEADS = 32
KEY_VALUE_HEADS = 4
HEAD_SIZE = 128
SUFFIX_SLOTS = 128
QUERY_WIDTH = 4096


def body(
    queries,
    row_prompt,
    prompt_prefix_keys,
    prompt_prefix_values,
    row_suffix_keys,
    row_suffix_values,
    suffix_lengths,
    w_out,
):
    groups = lax.axis_size("grp")
    shards = lax.axis_size("seq")
    mine = lax.axis_index("seq")
    row_grp, width_dev = queries.shape
    capacity = 2 * row_grp // groups
    heads_dev = QUERY_HEADS // shards
    head_group = QUERY_HEADS // KEY_VALUE_HEADS
    factor = 1.0 / math.sqrt(HEAD_SIZE)
    row_query = lax.all_to_all(queries, "seq", split_axis=0, concat_axis=1, tiled=True)
    prompt_index = row_prompt[:, 0]
    order = jnp.arange(row_grp, dtype=jnp.int32)
    earlier = (prompt_index[:, None] == prompt_index[None, :]) & (order[:, None] > order[None, :])
    rank = jnp.sum(earlier.astype(jnp.int32), axis=1)
    target = prompt_index * capacity + rank
    placing = (jnp.arange(groups * capacity, dtype=jnp.int32)[:, None] == target[None, :]).astype(
        jnp.bfloat16
    )
    packed = jnp.dot(placing, queries, preferred_element_type=jnp.float32).astype(jnp.bfloat16)
    arrived = lax.all_to_all(packed, "grp", split_axis=0, concat_axis=0, tiled=True)
    gathered_rows = lax.all_gather(arrived, "seq", axis=1, tiled=True)
    slot_positions = gathered_rows.shape[0]
    query_layout = gathered_rows.reshape(slot_positions, KEY_VALUE_HEADS, head_group, HEAD_SIZE)
    key_rows = prompt_prefix_keys[0].reshape(-1, KEY_VALUE_HEADS, HEAD_SIZE)
    value_rows = prompt_prefix_values[0].reshape(-1, KEY_VALUE_HEADS, HEAD_SIZE)
    scores = (
        jnp.einsum("nkgd,tkd->nkgt", query_layout, key_rows, preferred_element_type=jnp.float32)
        * factor
    )
    local_top = jnp.max(scores, axis=-1)
    top = lax.pmax(local_top, "seq")
    weights = jnp.exp(scores - top[..., None]).astype(jnp.bfloat16)
    total = jnp.sum(weights, axis=-1, dtype=jnp.float32).reshape(slot_positions, QUERY_HEADS)
    partial_value = jnp.einsum(
        "nkgt,tkd->nkgd", weights, value_rows, preferred_element_type=jnp.float32
    ).reshape(slot_positions, QUERY_WIDTH)
    top = top.reshape(slot_positions, QUERY_HEADS)
    total = lax.psum(total, "seq")
    out_part = lax.psum_scatter(
        partial_value.astype(jnp.bfloat16), "seq", scatter_dimension=1, tiled=True
    ).astype(jnp.float32)
    top_mine = lax.dynamic_slice_in_dim(top, mine * heads_dev, heads_dev, 1)
    total_mine = lax.dynamic_slice_in_dim(total, mine * heads_dev, heads_dev, 1)
    back_top, back_total, back_out = (
        lax.all_to_all(top_mine, "grp", split_axis=0, concat_axis=0, tiled=True),
        lax.all_to_all(total_mine, "grp", split_axis=0, concat_axis=0, tiled=True),
        lax.all_to_all(out_part, "grp", split_axis=0, concat_axis=0, tiled=True),
    )
    pre_top = jnp.take(back_top, target, axis=0)
    pre_total = jnp.take(back_total, target, axis=0)
    pre_out = jnp.take(back_out, target, axis=0)
    per_device = row_query.shape[0]
    suffix_query_rows = row_query.reshape(per_device, KEY_VALUE_HEADS, head_group, HEAD_SIZE)
    suffix_key_rows = row_suffix_keys.reshape(per_device, SUFFIX_SLOTS, KEY_VALUE_HEADS, HEAD_SIZE)
    suffix_value_rows = row_suffix_values.reshape(
        per_device, SUFFIX_SLOTS, KEY_VALUE_HEADS, HEAD_SIZE
    )
    live = (jnp.arange(SUFFIX_SLOTS, dtype=jnp.int32)[None, :] < suffix_lengths[:, None])[
        :, None, None, :
    ]
    sscores = (
        jnp.einsum(
            "vhfj,vahj->vhfa",
            suffix_query_rows,
            suffix_key_rows,
            preferred_element_type=jnp.float32,
        )
        * factor
    )
    sscores = jnp.where(live, sscores, -1e30)
    suf_max = jnp.max(sscores, axis=-1)
    sweights = jnp.where(live, jnp.exp(sscores - suf_max[..., None]), 0.0).astype(jnp.bfloat16)
    suf_total = jnp.sum(sweights, axis=-1, dtype=jnp.float32).reshape(per_device, QUERY_HEADS)
    suf_out = jnp.einsum(
        "rkgt,rtkd->rkgd", sweights, suffix_value_rows, preferred_element_type=jnp.float32
    ).reshape(per_device, QUERY_WIDTH)
    suf_max = suf_max.reshape(per_device, QUERY_HEADS)
    suf_top, suf_sum, suf_vals = (
        lax.all_to_all(suf_max, "seq", split_axis=1, concat_axis=0, tiled=True),
        lax.all_to_all(suf_total, "seq", split_axis=1, concat_axis=0, tiled=True),
        lax.all_to_all(suf_out, "seq", split_axis=1, concat_axis=0, tiled=True),
    )
    peak = jnp.maximum(pre_top, suf_top)
    left = jnp.exp(pre_top - peak)
    right = jnp.exp(suf_top - peak)
    denom = pre_total * left + suf_sum * right
    numer = (
        pre_out.reshape(row_grp, heads_dev, HEAD_SIZE) * left[..., None]
        + suf_vals.reshape(row_grp, heads_dev, HEAD_SIZE) * right[..., None]
    )
    attended = (numer / denom[..., None]).reshape(row_grp, width_dev).astype(jnp.bfloat16)
    projected = jnp.dot(attended, w_out, preferred_element_type=jnp.float32)
    return lax.psum_scatter(projected.astype(jnp.bfloat16), "seq", scatter_dimension=1, tiled=True)


def solution(mesh):
    in_specs = (
        P("grp", "seq"),
        P("grp", None),
        P("grp", "seq", None),
        P("grp", "seq", None),
        P(("grp", "seq"), None, None),
        P(("grp", "seq"), None, None),
        P(("grp", "seq")),
        P("seq", None),
    )
    out_specs = P("grp", "seq")
    return jax.shard_map(body, mesh=mesh, in_specs=in_specs, out_specs=out_specs, check_vma=False)
```

profile of v0, /device:TPU:1, one launch (start us, length us, event | category | flops | bytes accessed | tf_op | source)
XLA Modules:
  0.0 550.2 jit_solution(1190267714305756706)
XLA Ops:
  6.5 1.0 convert_reduce_fusion.2
  7.5 0.7 compare_select_fusion
  8.2 0.8 fusion.3
  9.1 27.1 %all_to_all.122 = bf16[16,8,128]{2,1,0:T(8,128)(2,1)} all-to-all(bf16[16,8,128]{2,1,0:T(8,128)(2,1)S(1)} %fusion.3), channel_id=1, replica_groups=mesh['grp'=16,'seq'=32] {'grp'}, dimensions={0} | all-to-all | bytes 65536 | tf_op jit(solution)/shard_map/all_to_all | solution.py:43
  36.2 9.1 %all-to-all-start.3 = ((bf16[32,2,128]{2,1,0:T(2,128)(2,1)}), bf16[32,2,128]{2,1,0:T(2,128)(2,1)S(1)}, u32[]{:S(2)}, u32[]{:S(2)}) async-start(bf16[32,2,128]{2,1,0:T(2,128)(2,1)} %bitcast.116), calls=%async_computation.3 | async-start | bytes 32768 | tf_op jit(solution)/shard_map/all_to_all | solution.py:33
  45.4 2.2 reshape_squeeze.6
  47.6 1.5 copy.71
  49.1 0.7 and_bitcast_fusion
  49.7 38.4 %all-gather.2.cloned.1.call-done = bf16[128,4096]{1,0:T(8,128)(2,1)} async-done(((bf16[128,128]{1,0:T(8,128)(2,1)}), bf16[128,4096]{1,0:T(8,128)(2,1)}) %all-gather.2.cloned.1.call-update) | async-done | bytes 1048592 | tf_op jit(solution)/shard_map/all_gather | solution.py:44
  88.2 2.3 copy.53
  90.5 9.9 %bitcast_reduce_fusion = (f32[128,4,8]{0,2,1:T(8,128)S(1)}, f32[4,128,8,1024]{3,1,2,0:T(8,128)}) fusion(bf16[128,4,8,128]{0,3,2,1:T(8,128)(2,1)} %bitcast.111, bf16[1024,4,128,1]{2,1,0,3:T(4,128)(2,1)} %bitcast.110), kind=kOutput, calls=%fused_computation.4 | convolution fusion | flops 1082126336 | bytes 18890752 | tf_op jit(solution)/shard_map/nkgd,tkd->nkgt/dot_general | solution.py:50
  100.4 120.9 %pmax.7 = f32[128,4,8]{0,2,1:T(8,128)S(1)} all-reduce(f32[128,4,8]{0,2,1:T(8,128)S(1)} %get-tuple-element.15), channel_id=1, replica_groups=mesh['grp'=16,'seq'=32] {'seq'}, use_global_device_ids=true, to_apply=%region_2.0 | all-reduce | flops 4096 | bytes 32768 | tf_op jit(solution)/shard_map/pmax | solution.py:54
  221.3 8.4 %convolution_convert_fusion.1 = bf16[4,128,8,128]{1,3,2,0:T(8,128)(2,1)} fusion(bf16[1024,4,128,1]{0,2,3,1:T(8,128)(2,1)S(1)} %bitcast.109, f32[4,128,8,1024]{3,1,2,0:T(8,128)} %get-tuple-element.16, f32[128,4,8]{0,2,1:T(8,128)S(1)} %pmax.7), kind=kOutput, calls=%fused_computation.9 | convolution fusion | flops 1086849024 | bytes 18890752 | tf_op jit(solution)/shard_map/nkgt,tkd->nkgd/dot_general | solution.py:57
  229.7 0.1 iota_compare_fusion.3
  229.8 0.3 fusion.29
  230.1 0.7 copy.72
  230.8 0.2 convert_reduce_fusion.1
  231.0 0.7 copy.73
  231.7 9.1 %all-to-all-start.7 = ((f32[2,32,1]{0,2,1:T(1,128)}), f32[2,32,1]{0,2,1:T(1,128)S(1)}, u32[]{:S(2)}, u32[]{:S(2)}) async-start(f32[2,32,1]{0,2,1:T(1,128)} %bitcast.32), calls=%async_computation.7 | async-start | bytes 32768 | tf_op jit(solution)/shard_map/all_to_all | solution.py:103
  240.8 7.7 %convert_reduce_fusion = f32[128,4,8]{0,2,1:T(8,128)S(1)} fusion(f32[128,4,8]{0,2,1:T(8,128)S(1)} %pmax.7, f32[4,128,8,1024]{3,1,2,0:T(8,128)} %get-tuple-element.16), kind=kLoop, calls=%fused_computation.7 | loop fusion | flops 20967424 | bytes 16809984 | tf_op jit(solution)/shard_map/reduce_sum | solution.py:56
  248.5 7.5 %all-to-all-start.4 = ((f32[2,32,1]{0,2,1:T(1,128)}), f32[2,32,1]{0,2,1:T(1,128)S(1)}, u32[]{:S(2)}, u32[]{:S(2)}) async-start(f32[2,32,1]{0,2,1:T(1,128)} %bitcast.22), calls=%async_computation.4 | async-start | bytes 32768 | tf_op jit(solution)/shard_map/all_to_all | solution.py:102
  256.0 123.3 %psum.7 = f32[128,32]{0,1:T(8,128)S(1)} all-reduce(f32[128,32]{0,1:T(8,128)S(1)} %bitcast.118), channel_id=1, replica_groups=mesh['grp'=16,'seq'=32] {'seq'}, use_global_device_ids=true, to_apply=%region_6.0 | all-reduce | flops 4096 | bytes 32768 | tf_op jit(solution)/shard_map/psum | solution.py:61
  379.3 0.7 all_to_all.106
  380.0 12.0 %all-to-all-start.6 = ((f32[16,8,1]{1,2,0:T(1,128)}), f32[16,8,1]{1,2,0:T(1,128)S(1)}, u32[]{:S(2)}, u32[]{:S(2)}) async-start(f32[16,8,1]{1,2,0:T(1,128)} %bitcast.30), calls=%async_computation.6 | async-start | bytes 16384 | tf_op jit(solution)/shard_map/all_to_all | solution.py:69
  392.1 0.7 all_to_all.93
  392.8 0.9 copy.75
  393.6 9.7 %all-to-all-done.6 = f32[16,8,1]{1,2,0:T(1,128)S(1)} async-done(((f32[16,8,1]{1,2,0:T(1,128)}), f32[16,8,1]{1,2,0:T(1,128)S(1)}, u32[]{:S(2)}, u32[]{:S(2)}) %all-to-all-start.6) | async-done | bytes 544 | tf_op jit(solution)/shard_map/all_to_all | solution.py:69
  403.3 3.5 all-to-all-start.2
  406.8 0.6 bitcast_convert_fusion
  407.4 10.5 %all-to-all-done.2 = f32[16,8,1]{1,2,0:T(1,128)S(1)} async-done(((f32[16,8,1]{1,2,0:T(1,128)}), f32[16,8,1]{1,2,0:T(1,128)S(1)}, u32[]{:S(2)}, u32[]{:S(2)}) %all-to-all-start.2) | async-done | bytes 544 | tf_op jit(solution)/shard_map/all_to_all | solution.py:68
  417.9 3.5 all-to-all-start.1
  421.5 0.2 convolution_bitcast_fusion
  421.7 0.7 copy.63
  422.4 0.1 all_to_all.112
  422.5 0.1 all_to_all.102
  422.6 0.5 broadcast.76
  423.2 0.6 reduce.22
  423.8 0.1 reshape.182
  423.9 0.6 reduce.23
  424.6 0.1 reshape.179
  424.6 0.8 gather_fusion.2
  425.4 0.8 gather_fusion.1
  426.2 6.8 %all-to-all-done.1 = f32[16,8,128]{2,1,0:T(8,128)S(1)} async-done(((f32[16,8,128]{2,1,0:T(8,128)}), f32[16,8,128]{2,1,0:T(8,128)S(1)}, u32[]{:S(2)}, u32[]{:S(2)}) %all-to-all-start.1) | async-done | bytes 65568 | tf_op jit(solution)/shard_map/all_to_all | solution.py:70
  433.0 12.8 %all-to-all-start.5 = ((f32[2,32,128]{2,0,1:T(2,128)}), f32[2,32,128]{2,0,1:T(2,128)S(1)}, u32[]{:S(2)}, u32[]{:S(2)}) async-start(f32[2,32,128]{2,0,1:T(2,128)} %copy.63), calls=%async_computation.5 | async-start | bytes 65536 | tf_op jit(solution)/shard_map/all_to_all | solution.py:104
  445.9 0.6 gather_fusion
  446.5 6.7 %all-to-all-done.5 = f32[2,32,128]{2,0,1:T(2,128)S(1)} async-done(((f32[2,32,128]{2,0,1:T(2,128)}), f32[2,32,128]{2,0,1:T(2,128)S(1)}, u32[]{:S(2)}, u32[]{:S(2)}) %all-to-all-start.5) | async-done | bytes 32800 | tf_op jit(solution)/shard_map/all_to_all | solution.py:104
  453.2 1.5 convolution_convert_fusion
  454.8 88.9 %reduce-scatter.5.cloned.1.call-done = bf16[64,256]{1,0:T(8,128)(2,1)} async-done(((bf16[64,8192]{1,0:T(8,128)(2,1)}), bf16[64,256]{1,0:T(8,128)(2,1)}) %reduce-scatter.5.cloned.1.call-update) | async-done | bytes 32784 | tf_op jit(solution)/shard_map/reduce_scatter | solution.py:116
  (25 shorter events, 0.3 us)
Async XLA Ops:
  6.5 446.7 %copy-start = (bf16[128,8192]{1,0:T(8,128)(2,1)S(1)}, bf16[128,8192]{1,0:T(8,128)(2,1)}, u32[]{:S(2)}) copy-start(bf16[128,8192]{1,0:T(8,128)(2,1)} %param.17) | copy-start | bytes 6291460
  6.5 81.6 %all-gather.2.cloned.1.call-start = ((), (), s32[]{:S(2)}) async-start(), calls=%async_computation.10 | async-start | bytes 1081344 | tf_op jit(solution)/shard_map/all_gather | solution.py:44
  36.2 193.5 %all-to-all-start.3 = ((bf16[32,2,128]{2,1,0:T(2,128)(2,1)}), bf16[32,2,128]{2,1,0:T(2,128)(2,1)S(1)}, u32[]{:S(2)}, u32[]{:S(2)}) async-start(bf16[32,2,128]{2,1,0:T(2,128)(2,1)} %bitcast.116), calls=%async_computation.3 | async-start | bytes 32768 | tf_op jit(solution)/shard_map/all_to_all | solution.py:33
  45.4 347.4 %reduce-scatter.7.cloned.1.call-start = ((), (), s32[]{:S(2)}) async-start(), calls=%async_computation.12 | async-start | bytes 1081344
  90.5 139.2 %copy-start.3 = (s32[2]{0:T(128)S(1)}, s32[2]{0:T(128)}, u32[]{:S(2)}) copy-start(s32[2]{0:T(128)} %param.16) | copy-start | bytes 28
  90.5 139.3 %copy-start.1 = (bf16[2,128,512]{2,1,0:T(8,128)(2,1)S(1)}, bf16[2,128,512]{2,1,0:T(8,128)(2,1)}, u32[]{:S(2)}) copy-start(bf16[2,128,512]{2,1,0:T(8,128)(2,1)} %param.14) | copy-start | bytes 786436
  229.6 191.8 %copy-start.2 = (bf16[2,128,512]{2,1,0:T(8,128)(2,1)S(1)}, bf16[2,128,512]{2,1,0:T(8,128)(2,1)}, u32[]{:S(2)}) copy-start(bf16[2,128,512]{2,1,0:T(8,128)(2,1)} %param.15) | copy-start | bytes 786436
  231.7 16.8 %all-to-all-start.7 = ((f32[2,32,1]{0,2,1:T(1,128)}), f32[2,32,1]{0,2,1:T(1,128)S(1)}, u32[]{:S(2)}, u32[]{:S(2)}) async-start(f32[2,32,1]{0,2,1:T(1,128)} %bitcast.32), calls=%async_computation.7 | async-start | bytes 32768 | tf_op jit(solution)/shard_map/all_to_all | solution.py:103
  248.5 131.5 %all-to-all-start.4 = ((f32[2,32,1]{0,2,1:T(1,128)}), f32[2,32,1]{0,2,1:T(1,128)S(1)}, u32[]{:S(2)}, u32[]{:S(2)}) async-start(f32[2,32,1]{0,2,1:T(1,128)} %bitcast.22), calls=%async_computation.4 | async-start | bytes 32768 | tf_op jit(solution)/shard_map/all_to_all | solution.py:102
  380.0 23.3 %all-to-all-start.6 = ((f32[16,8,1]{1,2,0:T(1,128)}), f32[16,8,1]{1,2,0:T(1,128)S(1)}, u32[]{:S(2)}, u32[]{:S(2)}) async-start(f32[16,8,1]{1,2,0:T(1,128)} %bitcast.30), calls=%async_computation.6 | async-start | bytes 16384 | tf_op jit(solution)/shard_map/all_to_all | solution.py:69
  403.3 14.6 %all-to-all-start.2 = ((f32[16,8,1]{1,2,0:T(1,128)}), f32[16,8,1]{1,2,0:T(1,128)S(1)}, u32[]{:S(2)}, u32[]{:S(2)}) async-start(f32[16,8,1]{1,2,0:T(1,128)} %bitcast.17), calls=%async_computation.2 | async-start | bytes 16384 | tf_op jit(solution)/shard_map/all_to_all | solution.py:68
  417.9 15.1 %all-to-all-start.1 = ((f32[16,8,128]{2,1,0:T(8,128)}), f32[16,8,128]{2,1,0:T(8,128)S(1)}, u32[]{:S(2)}, u32[]{:S(2)}) async-start(f32[16,8,128]{2,1,0:T(8,128)} %bitcast_convert_fusion), calls=%async_computation.1 | async-start | bytes 131072 | tf_op jit(solution)/shard_map/all_to_all | solution.py:70
  433.0 20.2 %all-to-all-start.5 = ((f32[2,32,128]{2,0,1:T(2,128)}), f32[2,32,128]{2,0,1:T(2,128)S(1)}, u32[]{:S(2)}, u32[]{:S(2)}) async-start(f32[2,32,128]{2,0,1:T(2,128)} %copy.63), calls=%async_computation.5 | async-start | bytes 65536 | tf_op jit(solution)/shard_map/all_to_all | solution.py:104
  445.8 97.8 %reduce-scatter.5.cloned.1.call-start = ((), (), s32[]{:S(2)}) async-start(), calls=%async_computation.11 | async-start | bytes 1081344 | tf_op jit(solution)/shard_map/reduce_scatter | solution.py:116
Sparse Core Ops, SparseCore 0:
  36.3 51.8 all-gather.1
  229.8 100.3 reduce-scatter.6
  454.9 88.7 reduce-scatter.4
where the time goes:
time: 551 us; the launch traced here: 550 us
  blocking collectives  271 us (49%)
  waiting for transfers between devices  161 us (29%)
  starting transfers between devices  57.6 us (10%)
  matrix products  21.2 us (4%)
  local copies, waits for them, and re-layouts  13.5 us (2%)
  between operations  13.3 us (2%)
  other arithmetic  12.2 us (2%)
    psum x1, blocking collectives, body(): total = lax.psum(total, 'seq')  123 us
    pmax x1, blocking collectives, body(): top = lax.pmax(local_top, 'seq')  121 us
    reduce_scatter x1, waiting for transfers between devices, body(): lax.psum_scatter(projected.astype(jnp.bfloat16), 'seq', scatter_dimension...  88.9 us
    all_gather x1, waiting for transfers between devices, body(): gathered_rows = lax.all_gather(arrived, 'seq', axis=1, tiled=True)  38.4 us
    all_to_all x1, blocking collectives, body(): lax.all_to_all(packed, 'grp', split_axis=0, concat_axis=0, tiled=True)  27.1 us
    all_to_all x1, starting transfers between devices, body(): lax.all_to_all(suf_out, 'seq', split_axis=1, concat_axis=0, tiled=True)  12.8 us
    all_to_all x1, starting transfers between devices, body(): lax.all_to_all(total_mine, 'grp', split_axis=0, concat_axis=0, tiled=True)  12 us
  transfers between devices with their start and end apart: 10, of which 6 were waited for; matrix products, arithmetic and copies ran while one was open for 7% of the time, Pallas kernels for 0%

commit v1 on v0

v1 whole, which is shorter than its diff:
```python
import math

import jax
import jax.numpy as jnp
from jax import lax
from jax.experimental import pallas as pl
from jax.experimental.pallas import tpu as pltpu
from jax.sharding import Mesh, PartitionSpec as P

QUERY_HEADS = 32
KEY_VALUE_HEADS = 4
HEAD_SIZE = 128
SUFFIX_SLOTS = 128
CAP = 8
PLANE = ("x", "y")
SWAP = ((0, 1), (1, 0))
TAIL = 16
FACTOR = 1.0 / math.sqrt(HEAD_SIZE)
LOG2E = 1.0 / math.log(2.0)
BIG = 48 * 1024 * 1024
F32, BF16 = jnp.float32, jnp.bfloat16


def iota(shape, dim):
    return lax.broadcasted_iota(jnp.int32, shape, dim)


def matmul(a, b, ca=1, cb=0):
    return lax.dot_general(a, b, (((ca,), (cb,)), ((), ())), preferred_element_type=F32)


def high_part(value):
    return value.astype(BF16).astype(F32)


def whole_spec(shape):
    return pl.BlockSpec(shape, lambda *_: (0,) * len(shape))


def pack_kernel(prompt_ref, query_ref, packed_ref, place_ref):
    prompt = prompt_ref[...]
    rows, slots = prompt.shape[0], packed_ref.shape[0]
    lanes = iota((rows, slots), 1)
    named = (lanes == prompt).astype(F32)
    lower = (iota((rows, rows), 0) > iota((rows, rows), 1)).astype(F32)
    before = matmul(lower.astype(BF16), named.astype(BF16))
    rank = jnp.sum(before * named, axis=1, keepdims=True).astype(jnp.int32)
    place = (lanes == prompt * CAP + rank).astype(F32).astype(BF16)
    place_ref[...] = place
    packed_ref[...] = matmul(place, query_ref[...], 0, 0).astype(BF16)


def pack(row_prompt, queries, slots):
    rows = queries.shape[0]
    return pl.pallas_call(
        pack_kernel,
        out_shape=(
            jax.ShapeDtypeStruct((slots, HEAD_SIZE), BF16),
            jax.ShapeDtypeStruct((rows, slots), BF16),
        ),
        name="pack",
    )(row_prompt, queries)


def attend_kernel(
    core_ref,
    own_len_ref,
    other_len_ref,
    here_ref,
    k0_ref,
    k1_ref,
    v0_ref,
    v1_ref,
    sk0_ref,
    sk1_ref,
    sv0_ref,
    sv1_ref,
    out_ref,
):
    heads = here_ref.shape[0]
    slots = here_ref.shape[1] - TAIL
    ones = jnp.ones((k0_ref.shape[0], HEAD_SIZE), BF16)
    v0 = jnp.concatenate([v0_ref[...], ones], axis=1)
    v1 = jnp.concatenate([v1_ref[...], ones], axis=1)
    k0, k1 = k0_ref[...], k1_ref[...]

    rows = heads * TAIL
    suffix_query = jnp.concatenate([here_ref[h, slots:, :] for h in range(heads)], axis=0)
    skeys = jnp.concatenate([sk0_ref[0], sk0_ref[1], sk1_ref[0], sk1_ref[1]], axis=0)
    svalues = jnp.concatenate([sv0_ref[0], sv0_ref[1], sv1_ref[0], sv1_ref[1]], axis=0)
    span = skeys.shape[0]
    scores = matmul(suffix_query, skeys, 1, 1)
    column = iota((rows, span), 1)
    block, place = column >> 7, column & 127
    length = jnp.where(
        block < 2,
        jnp.where(block == 0, own_len_ref[0], own_len_ref[1]),
        jnp.where(block == 2, other_len_ref[0], other_len_ref[1]),
    )
    line = iota((rows, span), 0) & 7
    live = (line == ((block + 2 * core_ref[0]) & 3)) & (place < length)
    peak = jnp.max(jnp.where(live, scores, -1e30), axis=1, keepdims=True)
    sshift = high_part(peak * FACTOR)
    sweights = jnp.where(live, jnp.exp2(scores * (FACTOR * LOG2E) - sshift * LOG2E), 0.0)
    sweights = sweights.astype(BF16)
    souts = matmul(
        sweights, jnp.concatenate([svalues, jnp.ones((span, HEAD_SIZE), BF16)], axis=1)
    )
    lane = iota((rows, HEAD_SIZE), 1)
    stotal = souts[:, HEAD_SIZE:]
    stotal_high = high_part(stotal)
    numbers = jnp.where(
        lane == 0,
        sshift,
        jnp.where(lane == 1, stotal_high, jnp.where(lane == 2, stotal - stotal_high, 0.0)),
    )
    tail_line = iota((rows, HEAD_SIZE), 0) & (TAIL - 1)
    tail = jnp.where(
        tail_line < 4,
        souts[:, :HEAD_SIZE],
        jnp.where((tail_line >= 8) & (tail_line < 12), numbers, 0.0),
    )

    lane = iota((2 * slots, HEAD_SIZE), 1)
    for pair in range(heads // 2):
        query = jnp.concatenate([here_ref[2 * pair + i, :slots, :] for i in range(2)], axis=0)
        s0 = matmul(query, k0, 1, 1)
        s1 = matmul(query, k1, 1, 1)
        peak = jnp.maximum(
            jnp.max(s0, axis=1, keepdims=True), jnp.max(s1, axis=1, keepdims=True)
        )
        shift = high_part(peak * FACTOR)
        low = shift * LOG2E
        w0 = jnp.exp2(s0 * (FACTOR * LOG2E) - low).astype(BF16)
        w1 = jnp.exp2(s1 * (FACTOR * LOG2E) - low).astype(BF16)
        outs = matmul(w0, v0) + matmul(w1, v1)
        total = outs[:, HEAD_SIZE:]
        total_high = high_part(total)
        numbers = jnp.where(
            lane == 4,
            shift,
            jnp.where(lane == 5, total_high, jnp.where(lane == 6, total - total_high, 0.0)),
        )
        for i in range(2):
            h = 2 * pair + i
            cut = slice(i * slots, (i + 1) * slots)
            out_ref[h, :slots, :] = outs[cut, :HEAD_SIZE].astype(BF16)
            across = numbers[cut].T[:TAIL]
            out_ref[h, slots:, :] = (tail[h * TAIL : (h + 1) * TAIL] + across).astype(BF16)


def attend(core, own_len, other_len, here, k0, k1, v0, v1, sk0, sk1, sv0, sv1):
    chips, height, _ = here.shape
    heads = chips // KEY_VALUE_HEADS
    length = k0.shape[0]
    smem = pl.BlockSpec(memory_space=pltpu.SMEM)
    chunk = pl.BlockSpec((heads, height, HEAD_SIZE), lambda j: (j, 0, 0))
    prefix = pl.BlockSpec((length, HEAD_SIZE), lambda j: (0, j))
    suffix = pl.BlockSpec((2, SUFFIX_SLOTS, HEAD_SIZE), lambda j: (0, 0, j))
    return pl.pallas_call(
        attend_kernel,
        grid=(KEY_VALUE_HEADS,),
        in_specs=[smem, smem, smem, chunk] + [prefix] * 4 + [suffix] * 4,
        out_specs=chunk,
        out_shape=jax.ShapeDtypeStruct(here.shape, BF16),
        compiler_params=pltpu.CompilerParams(vmem_limit_bytes=BIG),
        cost_estimate=pl.CostEstimate(
            flops=4 * chips * height * 2 * length * HEAD_SIZE,
            bytes_accessed=10 * length * KEY_VALUE_HEADS * HEAD_SIZE,
            transcendentals=chips * height * 2 * length,
        ),
        name="attend",
    )(core, own_len, other_len, here, k0, k1, v0, v1, sk0, sk1, sv0, sv1)


def merge_kernel(own_ref, sent_ref):
    chips, height, _ = own_ref.shape
    slots, groups = height - TAIL, sent_ref.shape[0]
    tails = own_ref[:, slots:, :].astype(F32)
    shift = tails[:, 4, :]
    total = tails[:, 5, :] + tails[:, 6, :]
    top = jnp.max(shift, axis=0, keepdims=True)
    scale = jnp.exp(shift - top)
    whole = jnp.sum(total * scale, axis=0, keepdims=True)
    whole_high = high_part(whole)
    line = iota((8, slots), 0)
    numbers = jnp.where(
        line == 0, top, jnp.where(line == 1, whole_high, jnp.where(line == 2, whole - whole_high, 0.0))
    )
    rest = jnp.zeros((HEAD_SIZE - chips - 8, slots), F32)
    across = jnp.concatenate([scale / whole, numbers, rest], axis=0).T
    mean = jnp.zeros((slots, HEAD_SIZE), F32)
    for k in range(chips):
        mean += across[:, k : k + 1] * own_ref[k, :slots, :].astype(F32)
    cap = slots // groups
    both = [value.reshape(groups, cap, HEAD_SIZE) for value in (mean, across)]
    sent_ref[...] = jnp.concatenate(both, axis=1).astype(BF16)


def merge(own, groups):
    cap = (own.shape[1] - TAIL) // groups
    return pl.pallas_call(
        merge_kernel,
        out_shape=jax.ShapeDtypeStruct((groups, 2 * cap, HEAD_SIZE), BF16),
        compiler_params=pltpu.CompilerParams(vmem_limit_bytes=BIG),
        name="merge",
    )(own)


def finish_kernel(first, place_ref, back_ref, tails_ref, attended_ref):
    groups, double, _ = back_ref.shape
    cap = double // 2
    rows = place_ref.shape[0]
    chips = tails_ref.shape[0]
    back = back_ref[...].astype(F32)
    means = back[:, :cap].reshape(groups * cap, HEAD_SIZE).astype(BF16)
    numbers = back[:, cap:].reshape(groups * cap, HEAD_SIZE).astype(BF16)
    place = place_ref[...]
    pre_mean = matmul(place, means)
    pre_numbers = matmul(place, numbers)
    pre_top = pre_numbers[:, first : first + 1]
    pre_total = pre_numbers[:, first + 1 : first + 2] + pre_numbers[:, first + 2 : first + 3]

    tails = tails_ref[...].reshape(chips * TAIL, HEAD_SIZE)
    row, column = iota((rows, chips * TAIL), 0), iota((rows, chips * TAIL), 1)
    spot = (row >> 2) * TAIL + (row & 3)
    suf_out = matmul((column == spot).astype(F32).astype(BF16), tails)
    suf_numbers = matmul((column == spot + 8).astype(F32).astype(BF16), tails)
    suf_top = suf_numbers[:, 0:1]
    suf_total = suf_numbers[:, 1:2] + suf_numbers[:, 2:3]

    peak = jnp.maximum(pre_top, suf_top)
    left = jnp.exp(pre_top - peak) * pre_total
    right = jnp.exp(suf_top - peak)
    attended = (pre_mean * left + suf_out * right) / (left + suf_total * right)
    attended_ref[...] = attended.astype(BF16)


def finish(place, back, own):
    chips, height, _ = own.shape
    rows = place.shape[0]
    return pl.pallas_call(
        lambda *refs: finish_kernel(chips, *refs),
        grid=(1,),
        in_specs=[
            whole_spec(place.shape),
            whole_spec(back.shape),
            pl.BlockSpec((chips, TAIL, HEAD_SIZE), lambda i: (0, height // TAIL - 1, 0)),
        ],
        out_specs=whole_spec((rows, HEAD_SIZE)),
        out_shape=jax.ShapeDtypeStruct((rows, HEAD_SIZE), BF16),
        name="finish",
    )(place, back, own)


def project_kernel(core_ref, a0_ref, a1_ref, w0_ref, w1_ref, out_ref):
    width = out_ref.shape[2]
    a0, a1 = a0_ref[...], a1_ref[...]
    for k in range(out_ref.shape[0]):
        start = pl.multiple_of(2 * width * k + core_ref[0] * width, width)
        columns = pl.ds(start, width)
        out_ref[k] = (matmul(a0, w0_ref[:, columns]) + matmul(a1, w1_ref[:, columns])).astype(BF16)


def project(core, a0, a1, w0, w1, chips):
    rows, feats = a0.shape
    width = w0.shape[1] // (2 * chips)
    steps = 2
    part = chips // steps
    weight = pl.BlockSpec((feats, 2 * width * part), lambda i: (0, i))
    return pl.pallas_call(
        project_kernel,
        grid=(steps,),
        in_specs=[
            pl.BlockSpec(memory_space=pltpu.SMEM),
            whole_spec(a0.shape),
            whole_spec(a1.shape),
            weight,
            weight,
        ],
        out_specs=pl.BlockSpec((part, rows, width), lambda i: (i, 0, 0)),
        out_shape=jax.ShapeDtypeStruct((chips, rows, width), BF16),
        compiler_params=pltpu.CompilerParams(vmem_limit_bytes=BIG),
        name="project",
    )(core, a0, a1, w0, w1)


def body(
    queries,
    row_prompt,
    prompt_prefix_keys,
    prompt_prefix_values,
    row_suffix_keys,
    row_suffix_values,
    suffix_lengths,
    w_out,
):
    groups = lax.axis_size("grp")
    chips = lax.axis_size("x") * lax.axis_size("y")
    core = lax.axis_index("core").reshape(1).astype(jnp.int32)
    row_grp = queries.shape[0]
    chip_rows = row_grp // chips
    slots = groups * CAP
    keys, values = prompt_prefix_keys[0], prompt_prefix_values[0]

    packed, place = pack(row_prompt, queries, slots)
    arrived = lax.all_to_all(packed, "grp", split_axis=0, concat_axis=0, tiled=True)

    held = (keys, values, row_suffix_keys, row_suffix_values, suffix_lengths, w_out)
    _, held = lax.optimization_barrier((packed, held))
    others = [lax.ppermute(value, "core", SWAP) for value in held]
    keys_other, values_other, skeys_other, svalues_other, lengths_other, w_other = others

    asked = queries.reshape(chips, chip_rows, HEAD_SIZE)
    gap = jnp.zeros((chips, 8 - chip_rows, HEAD_SIZE), BF16)
    spread = jnp.concatenate(
        [jnp.broadcast_to(arrived[None], (chips, slots, HEAD_SIZE)), asked, gap, asked, gap],
        axis=1,
    )
    here = lax.all_to_all(spread, PLANE, split_axis=0, concat_axis=0, tiled=True)

    parts = attend(
        core,
        suffix_lengths,
        lengths_other,
        here,
        keys,
        keys_other,
        values,
        values_other,
        row_suffix_keys,
        skeys_other,
        row_suffix_values,
        svalues_other,
    )
    own = lax.all_to_all(parts, PLANE, split_axis=0, concat_axis=0, tiled=True)

    sent = merge(own, groups)
    back = lax.all_to_all(sent, "grp", split_axis=0, concat_axis=0, tiled=True)
    attended = finish(place, back, own)
    attended_other = lax.ppermute(attended, "core", SWAP)
    shares = project(core, attended, attended_other, w_out, w_other, chips)
    shares = lax.all_to_all(shares, PLANE, split_axis=0, concat_axis=0, tiled=True)
    return jnp.sum(shares.astype(F32), axis=0).astype(BF16)


def solution(mesh):
    side = math.isqrt(mesh.shape["seq"] // 2)
    fine = Mesh(
        mesh.devices.reshape(mesh.shape["grp"], side, side, 2), ("grp", "x", "y", "core")
    )
    seq = ("x", "y", "core")
    every = ("grp",) + seq
    in_specs = (
        P("grp", seq),
        P("grp", None),
        P("grp", seq, None),
        P("grp", seq, None),
        P(every, None, None),
        P(every, None, None),
        P(every),
        P(seq, None),
    )
    return jax.shard_map(
        body, mesh=fine, in_specs=in_specs, out_specs=P("grp", seq), check_vma=False
    )
```

time: 551 us -> 128 us (0.23)
  blocking collectives: 271 us -> 67.4 us
  waiting for transfers between devices: 161 us -> 2.47 us
  starting transfers between devices: 57.6 us -> 32.5 us
  matrix products: 21.2 us -> 0 us
  Pallas kernels: 0 us -> 16.9 us
  between operations: 13.3 us -> 0.18 us
  other arithmetic: 12.2 us -> 0.69 us
  local copies, waits for them, and re-layouts: 13.5 us -> 6.5 us
    psum x1 -> x0, blocking collectives: 123 us -> none  [body(): total = lax.psum(total, 'seq')]
    pmax x1 -> x0, blocking collectives: 121 us -> none  [body(): top = lax.pmax(local_top, 'seq')]
    reduce_scatter x1 -> x0, waiting for transfers between devices: 88.9 us -> none  [body(): lax.psum_scatter(projected.astype(jnp.bfloat16), 'seq', scatter_dimension...]
    all_to_all x7 -> x1, starting transfers between devices: 57.6 us -> 6.75 us  [body(): lax.all_to_all(spread, PLANE, split_axis=0, concat_axis=0, tiled=True)]
    all_to_all x0 -> x3, blocking collectives: none -> 46.4 us  [the longest x1 18.2 us: body(): own = lax.all_to_all(parts, PLANE, split_axis=0, concat_axis=0, tiled=True)]
    all_gather x1 -> x0, waiting for transfers between devices: 38.4 us -> none  [body(): gathered_rows = lax.all_gather(arrived, 'seq', axis=1, tiled=True)]
    all_to_all x7 -> x1, waiting for transfers between devices: 33.8 us -> 0.17 us  [body(): lax.all_to_all(spread, PLANE, split_axis=0, concat_axis=0, tiled=True)]
    ppermute x0 -> x7, starting transfers between devices: none -> 25.7 us  [the longest x6 21 us: body(): others = [lax.ppermute(value, 'core', SWAP) for value in held]]
  transfers between devices with their start and end apart: 10 -> 8, of which waited for: 6 -> 3; matrix products, arithmetic and copies ran while one was open for 7% -> 3% of each run, Pallas kernels for 0% -> 10%
where the time goes in v1:
time: 128 us; the launch traced here: 127 us
  blocking collectives  67.4 us (53%)
  starting transfers between devices  32.5 us (25%)
  Pallas kernels  16.9 us (13%)
  local copies, waits for them, and re-layouts  6.5 us (5%)
  waiting for transfers between devices  2.47 us (2%)
    all_to_all x1, blocking collectives, body(): lax.all_to_all(packed, 'grp', split_axis=0, concat_axis=0, tiled=True)  21 us
    ppermute x6, starting transfers between devices, body(): others = [lax.ppermute(value, 'core', SWAP) for value in held]  21 us
    all_to_all x1, blocking collectives, body(): own = lax.all_to_all(parts, PLANE, split_axis=0, concat_axis=0, tiled=True)  18.2 us
    all_to_all x1, blocking collectives, body(): back = lax.all_to_all(sent, 'grp', split_axis=0, concat_axis=0, tiled=True)  14.9 us
    all_to_all x1, blocking collectives, body(): lax.all_to_all(shares, PLANE, split_axis=0, concat_axis=0, tiled=True)  13.2 us
    pallas_call x1, Pallas kernels, attend(): pl.pallas_call(attend_kernel, grid=(KEY_VALUE_HEADS,), in_specs=[smem, sm...  10.5 us
    all_to_all x1, starting transfers between devices, body(): lax.all_to_all(spread, PLANE, split_axis=0, concat_axis=0, tiled=True)  6.75 us
    ppermute x1, starting transfers between devices, body(): attended_other = lax.ppermute(attended, 'core', SWAP)  4.76 us
  transfers between devices with their start and end apart: 8, of which 3 were waited for; matrix products, arithmetic and copies ran while one was open for 3% of the time, Pallas kernels for 10%

profile of v1, /device:TPU:1, one launch (start us, length us, event | category | flops | bytes accessed | tf_op | source)
XLA Modules:
  0.0 126.6 jit_solution(9488320166960779697)
XLA Ops:
  0.0 0.0 copy-start.7
  0.0 0.0 copy-start.6
  0.0 0.0 copy-start.5
  0.0 0.0 copy-start.4
  0.0 0.0 copy-start.3
  0.0 1.5 %copy.9.prompt_ref = s32[64,1]{1,0:T(8,128)} copy(s32[64,1]{0,1:T(1,128)} %param.9) | data formatting | bytes 512 | tf_op args[1]
  1.5 1.9 %pack.1 = (bf16[128,128]{1,0:T(8,128)(2,1)}, bf16[64,128]{1,0:T(8,128)(2,1)}) custom-call(s32[64,1]{1,0:T(8,128)} %copy.9.prompt_ref, bf16[64,128]{1,0:T(8,128)(2,1)} %query_ref.1), custom_call_target="tpu_custom_call" | custom-call | tf_op jit(solution)/shard_map/pack/pallas_call | solution.py:55
  3.4 8.8 %collective-permute-start.6 = (bf16[128,8192]{1,0:T(8,128)(2,1)}, bf16[128,8192]{1,0:T(8,128)(2,1)}, u32[]{:S(2)}, u32[]{:S(2)}) collective-permute-start(bf16[128,8192]{1,0:T(8,128)(2,1)} %w0_ref.1), channel_id=1, source_target_pairs={{0,1},{1,0},{2,3},{3,2},{4,5},{5,4},{6,7},{7,6},{8,9},{9,8},{10,11... | collective-permute-start | bytes 6291464 | tf_op jit(solution)/shard_map/ppermute | solution.py:311
  12.2 1.9 %collective-permute-start.1 = (bf16[1024,512]{1,0:T(8,128)(2,1)}, bf16[1024,512]{1,0:T(8,128)(2,1)}, u32[]{:S(2)}, u32[]{:S(2)}) collective-permute-start(bf16[1024,512]{1,0:T(8,128)(2,1)} %bitcast.6), channel_id=1, source_target_pairs={{0,1},{1,0},{2,3},{3,2},{4,5},{5,4},{6,7},{7,6},{8,9},{9,8},{10,11... | collective-permute-start | bytes 3145736 | tf_op jit(solution)/shard_map/ppermute | solution.py:311
  14.1 2.4 %collective-permute-start.2 = (bf16[1024,512]{1,0:T(8,128)(2,1)}, bf16[1024,512]{1,0:T(8,128)(2,1)}, u32[]{:S(2)}, u32[]{:S(2)}) collective-permute-start(bf16[1024,512]{1,0:T(8,128)(2,1)} %bitcast.8), channel_id=1, source_target_pairs={{0,1},{1,0},{2,3},{3,2},{4,5},{5,4},{6,7},{7,6},{8,9},{9,8},{10,11... | collective-permute-start | bytes 3145736 | tf_op jit(solution)/shard_map/ppermute | solution.py:311
  16.6 21.0 %all_to_all.29 = bf16[16,8,128]{2,1,0:T(8,128)(2,1)S(1)} all-to-all(bf16[16,8,128]{2,1,0:T(8,128)(2,1)} %bitcast.13), channel_id=1, replica_groups=mesh['grp'=16,'x'=4,'y'=4,'core'=2] {'grp'}, dimensions={0} | all-to-all | bytes 65536 | tf_op jit(solution)/shard_map/all_to_all | solution.py:307
  37.6 0.1 broadcast_in_dim.12
  37.7 4.1 %concatenate.3 = bf16[16,144,128]{2,1,0:T(8,128)(2,1)} concatenate(bf16[16,128,128]{2,1,0:T(8,128)(2,1)S(1)} %broadcast_in_dim.12, bf16[16,4,128]{2,1,0:T(4,128)(2,1)} %bitcast.10, bf16[16,4,128]{2,1,0:T(4,128)(2,1)S(1)} %broadcast_in_dim.13, bf16[16,4,128]{2,1,0:T(4,128)(2,1)} %bitcast.11, bf16[16,4,128]{2,1,0:T(4,128)(2,1)S(1)} %broadcast_in_dim.13), dimensions={1} | concatenate | bytes 1179648 | tf_op jit(solution)/shard_map/concatenate | solution.py:316
  41.9 6.8 %all-to-all-start.1 = ((bf16[16,144,128]{2,1,0:T(8,128)(2,1)}), bf16[16,144,128]{2,1,0:T(8,128)(2,1)S(1)}, u32[]{:S(2)}, u32[]{:S(2)}) async-start(bf16[16,144,128]{2,1,0:T(8,128)(2,1)} %concatenate.3), calls=%async_computation.1 | async-start | bytes 1179648 | tf_op jit(solution)/shard_map/all_to_all | solution.py:320
  48.6 0.0 copy-done.7
  48.6 3.6 %collective-permute-start = (s32[2]{0:T(128)S(1)}, s32[2]{0:T(128)S(1)}, u32[]{:S(2)}, u32[]{:S(2)}) collective-permute-start(s32[2]{0:T(128)S(1)} %copy-done.7), channel_id=1, source_target_pairs={{0,1},{1,0},{2,3},{3,2},{4,5},{5,4},{6,7},{7,6},{8,9},{9,8},{10,11... | collective-permute-start | bytes 32 | tf_op jit(solution)/shard_map/ppermute | solution.py:311
  52.2 0.0 copy-done.5
  52.2 1.9 %collective-permute-start.3 = (bf16[2,128,512]{2,1,0:T(8,128)(2,1)S(1)}, bf16[2,128,512]{2,1,0:T(8,128)(2,1)S(1)}, u32[]{:S(2)}, u32[]{:S(2)}) collective-permute-start(bf16[2,128,512]{2,1,0:T(8,128)(2,1)S(1)} %copy-done.5), channel_id=1, source_target_pairs={{0,1},{1,0},{2,3},{3,2},{4,5},{5,4},{6,7},{7,6},{8,9},{9,8},{10,11... | collective-permute-start | bytes 786440 | tf_op jit(solution)/shard_map/ppermute | solution.py:311
  54.1 0.0 collective-permute-done.other_len_ref
  54.1 0.0 copy-done.6
  54.2 2.4 %collective-permute-start.4 = (bf16[2,128,512]{2,1,0:T(8,128)(2,1)S(1)}, bf16[2,128,512]{2,1,0:T(8,128)(2,1)}, u32[]{:S(2)}, u32[]{:S(2)}) collective-permute-start(bf16[2,128,512]{2,1,0:T(8,128)(2,1)S(1)} %copy-done.6), channel_id=1, source_target_pairs={{0,1},{1,0},{2,3},{3,2},{4,5},{5,4},{6,7},{7,6},{8,9},{9,8},{10,11... | collective-permute-start | bytes 786440 | tf_op jit(solution)/shard_map/ppermute | solution.py:311
  56.6 0.0 collective-permute-done.3.sk1_ref
  56.6 1.3 collective-permute-done.4.sv1_ref
  57.8 0.2 all-to-all-done.1.here_ref
  58.0 0.0 collective-permute-done.1.k1_ref
  58.0 0.0 collective-permute-done.2.v1_ref
  58.0 0.0 copy-done.4
  58.0 0.0 copy-done.3
  58.0 10.5 %attend.1 = bf16[16,144,128]{2,1,0:T(8,128)(2,1)S(1)} custom-call(s32[1]{0:T(128)} %bitcast.core_ref, s32[2]{0:T(128)S(1)} %copy-done.7, s32[2]{0:T(128)S(1)} %collective-permute-done.other_len_ref, bf16[16,144,128]{2,1,0:T(8,128)(2,1)S(1)} %all-to-all-done.1.here_ref, bf16[1024,512]{1,0:T(8,128)(2,1)S(1)} %bitcast.7, ...), custom_call_target="tpu_custom_call" | custom-call | flops 2415919104 | bytes 5242880 | tf_op jit(solution)/shard_map/attend/pallas_call | solution.py:160
  68.5 0.0 copy-start.1
  68.5 18.2 %all_to_all.30.own_ref.refs_2_ = bf16[16,144,128]{2,1,0:T(8,128)(2,1)S(1)} all-to-all(bf16[16,144,128]{2,1,0:T(8,128)(2,1)S(1)} %attend.1), channel_id=1, replica_groups=mesh['grp'=16,'x'=4,'y'=4,'core'=2] {'x','y'}, dimensions={0} | all-to-all | bytes 1179648 | tf_op jit(solution)/shard_map/all_to_all | solution.py:336
  86.7 0.0 copy-start
  86.7 0.5 merge.1
  87.3 14.9 %all_to_all.31.refs_1_ = bf16[16,16,128]{2,1,0:T(8,128)(2,1)} all-to-all(bf16[16,16,128]{2,1,0:T(8,128)(2,1)S(1)} %merge.1), channel_id=1, replica_groups=mesh['grp'=16,'x'=4,'y'=4,'core'=2] {'grp'}, dimensions={0} | all-to-all | bytes 131072 | tf_op jit(solution)/shard_map/all_to_all | solution.py:339
  102.2 0.0 copy-done
  102.2 2.0 %finish.1.a0_ref = bf16[64,128]{1,0:T(8,128)(2,1)} custom-call(bf16[64,128]{1,0:T(8,128)(2,1)} %get-tuple-element.13.refs_0_, bf16[16,16,128]{2,1,0:T(8,128)(2,1)} %all_to_all.31.refs_1_, bf16[16,144,128]{2,1,0:T(8,128)(2,1)} %copy-done), custom_call_target="tpu_custom_call" | custom-call | tf_op jit(solution)/shard_map/finish/pallas_call | solution.py:242
  104.2 4.8 %collective-permute-start.5 = (bf16[64,128]{1,0:T(8,128)(2,1)}, bf16[64,128]{1,0:T(8,128)(2,1)S(1)}, u32[]{:S(2)}, u32[]{:S(2)}) collective-permute-start(bf16[64,128]{1,0:T(8,128)(2,1)} %finish.1.a0_ref), channel_id=1, source_target_pairs={{0,1},{1,0},{2,3},{3,2},{4,5},{5,4},{6,7},{7,6},{8,9},{9,8},{10,11... | collective-permute-start | bytes 49160 | tf_op jit(solution)/shard_map/ppermute | solution.py:341
  109.0 1.0 collective-permute-done.5.a1_ref
  110.0 0.0 collective-permute-done.6.w1_ref
  110.0 0.0 copy-done.1
  110.0 0.0 copy-start.2
  110.0 0.7 copy-done.2
  110.7 1.9 %project.1 = bf16[16,64,256]{2,1,0:T(8,128)(2,1)S(1)} custom-call(s32[1]{0:T(128)} %bitcast.core_ref, bf16[64,128]{1,0:T(8,128)(2,1)S(1)} %copy-done.2, bf16[64,128]{1,0:T(8,128)(2,1)S(1)} %collective-permute-done.5.a1_ref, bf16[128,8192]{1,0:T(8,128)(2,1)S(1)} %copy-done.1, bf16[128,8192]{1,0:T(8,128)(2,1)} %collective-permute-done.6.w1_ref), custom_call_target="tpu_custom_call" | custom-call | tf_op jit(solution)/shard_map/project/pallas_call | solution.py:271
  112.7 13.2 %all_to_all.32 = bf16[16,64,256]{2,1,0:T(8,128)(2,1)S(1)} all-to-all(bf16[16,64,256]{2,1,0:T(8,128)(2,1)S(1)} %project.1), channel_id=1, replica_groups=mesh['grp'=16,'x'=4,'y'=4,'core'=2] {'x','y'}, dimensions={0} | all-to-all | bytes 1048576 | tf_op jit(solution)/shard_map/all_to_all | solution.py:343
  125.9 0.7 reduce_sum.12
  (1 shorter events, 0.0 us)
Async XLA Ops:
  0.0 48.6 %copy-start.7 = (s32[2]{0:T(128)S(1)}, s32[2]{0:T(128)}, u32[]{:S(2)}) copy-start(s32[2]{0:T(128)} %own_len_ref.1) | copy-start | bytes 28
  0.0 54.1 %copy-start.6 = (bf16[2,128,512]{2,1,0:T(8,128)(2,1)S(1)}, bf16[2,128,512]{2,1,0:T(8,128)(2,1)}, u32[]{:S(2)}) copy-start(bf16[2,128,512]{2,1,0:T(8,128)(2,1)} %sv0_ref.1) | copy-start | bytes 786436
  0.0 52.2 %copy-start.5 = (bf16[2,128,512]{2,1,0:T(8,128)(2,1)S(1)}, bf16[2,128,512]{2,1,0:T(8,128)(2,1)}, u32[]{:S(2)}) copy-start(bf16[2,128,512]{2,1,0:T(8,128)(2,1)} %sk0_ref.1) | copy-start | bytes 786436
  0.0 58.0 %copy-start.4 = (bf16[1,1024,512]{2,1,0:T(8,128)(2,1)S(1)}, bf16[1,1024,512]{2,1,0:T(8,128)(2,1)}, u32[]{:S(2)}) copy-start(bf16[1,1024,512]{2,1,0:T(8,128)(2,1)} %param.11) | copy-start | bytes 3145732
  0.0 58.0 %copy-start.3 = (bf16[1,1024,512]{2,1,0:T(8,128)(2,1)S(1)}, bf16[1,1024,512]{2,1,0:T(8,128)(2,1)}, u32[]{:S(2)}) copy-start(bf16[1,1024,512]{2,1,0:T(8,128)(2,1)} %param.10) | copy-start | bytes 3145732
  3.4 106.6 %collective-permute-start.6 = (bf16[128,8192]{1,0:T(8,128)(2,1)}, bf16[128,8192]{1,0:T(8,128)(2,1)}, u32[]{:S(2)}, u32[]{:S(2)}) collective-permute-start(bf16[128,8192]{1,0:T(8,128)(2,1)} %w0_ref.1), channel_id=1, source_target_pairs={{0,1},{1,0},{2,3},{3,2},{4,5},{5,4},{6,7},{7,6},{8,9},{9,8},{10,11... | collective-permute-start | bytes 6291464 | tf_op jit(solution)/shard_map/ppermute | solution.py:311
  12.2 45.8 %collective-permute-start.1 = (bf16[1024,512]{1,0:T(8,128)(2,1)}, bf16[1024,512]{1,0:T(8,128)(2,1)}, u32[]{:S(2)}, u32[]{:S(2)}) collective-permute-start(bf16[1024,512]{1,0:T(8,128)(2,1)} %bitcast.6), channel_id=1, source_target_pairs={{0,1},{1,0},{2,3},{3,2},{4,5},{5,4},{6,7},{7,6},{8,9},{9,8},{10,11... | collective-permute-start | bytes 3145736 | tf_op jit(solution)/shard_map/ppermute | solution.py:311
  14.1 43.9 %collective-permute-start.2 = (bf16[1024,512]{1,0:T(8,128)(2,1)}, bf16[1024,512]{1,0:T(8,128)(2,1)}, u32[]{:S(2)}, u32[]{:S(2)}) collective-permute-start(bf16[1024,512]{1,0:T(8,128)(2,1)} %bitcast.8), channel_id=1, source_target_pairs={{0,1},{1,0},{2,3},{3,2},{4,5},{5,4},{6,7},{7,6},{8,9},{9,8},{10,11... | collective-permute-start | bytes 3145736 | tf_op jit(solution)/shard_map/ppermute | solution.py:311
  41.9 16.2 %all-to-all-start.1 = ((bf16[16,144,128]{2,1,0:T(8,128)(2,1)}), bf16[16,144,128]{2,1,0:T(8,128)(2,1)S(1)}, u32[]{:S(2)}, u32[]{:S(2)}) async-start(bf16[16,144,128]{2,1,0:T(8,128)(2,1)} %concatenate.3), calls=%async_computation.1 | async-start | bytes 1179648 | tf_op jit(solution)/shard_map/all_to_all | solution.py:320
  48.6 5.5 %collective-permute-start = (s32[2]{0:T(128)S(1)}, s32[2]{0:T(128)S(1)}, u32[]{:S(2)}, u32[]{:S(2)}) collective-permute-start(s32[2]{0:T(128)S(1)} %copy-done.7), channel_id=1, source_target_pairs={{0,1},{1,0},{2,3},{3,2},{4,5},{5,4},{6,7},{7,6},{8,9},{9,8},{10,11... | collective-permute-start | bytes 32 | tf_op jit(solution)/shard_map/ppermute | solution.py:311
  52.2 4.4 %collective-permute-start.3 = (bf16[2,128,512]{2,1,0:T(8,128)(2,1)S(1)}, bf16[2,128,512]{2,1,0:T(8,128)(2,1)S(1)}, u32[]{:S(2)}, u32[]{:S(2)}) collective-permute-start(bf16[2,128,512]{2,1,0:T(8,128)(2,1)S(1)} %copy-done.5), channel_id=1, source_target_pairs={{0,1},{1,0},{2,3},{3,2},{4,5},{5,4},{6,7},{7,6},{8,9},{9,8},{10,11... | collective-permute-start | bytes 786440 | tf_op jit(solution)/shard_map/ppermute | solution.py:311
  54.2 3.7 %collective-permute-start.4 = (bf16[2,128,512]{2,1,0:T(8,128)(2,1)S(1)}, bf16[2,128,512]{2,1,0:T(8,128)(2,1)}, u32[]{:S(2)}, u32[]{:S(2)}) collective-permute-start(bf16[2,128,512]{2,1,0:T(8,128)(2,1)S(1)} %copy-done.6), channel_id=1, source_target_pairs={{0,1},{1,0},{2,3},{3,2},{4,5},{5,4},{6,7},{7,6},{8,9},{9,8},{10,11... | collective-permute-start | bytes 786440 | tf_op jit(solution)/shard_map/ppermute | solution.py:311
  68.5 41.5 %copy-start.1 = (bf16[128,8192]{1,0:T(8,128)(2,1)S(1)}, bf16[128,8192]{1,0:T(8,128)(2,1)}, u32[]{:S(2)}) copy-start(bf16[128,8192]{1,0:T(8,128)(2,1)} %w0_ref.1) | copy-start | bytes 6291460
  86.7 15.4 %copy-start = (bf16[16,144,128]{2,1,0:T(8,128)(2,1)}, bf16[16,144,128]{2,1,0:T(8,128)(2,1)S(1)}, u32[]{:S(2)}) copy-start(bf16[16,144,128]{2,1,0:T(8,128)(2,1)S(1)} %all_to_all.30.own_ref.refs_2_) | copy-start | bytes 1769476
  104.2 5.8 %collective-permute-start.5 = (bf16[64,128]{1,0:T(8,128)(2,1)}, bf16[64,128]{1,0:T(8,128)(2,1)S(1)}, u32[]{:S(2)}, u32[]{:S(2)}) collective-permute-start(bf16[64,128]{1,0:T(8,128)(2,1)} %finish.1.a0_ref), channel_id=1, source_target_pairs={{0,1},{1,0},{2,3},{3,2},{4,5},{5,4},{6,7},{7,6},{8,9},{9,8},{10,11... | collective-permute-start | bytes 49160 | tf_op jit(solution)/shard_map/ppermute | solution.py:341
  110.0 0.7 copy-start.2

commit v2 on v1

v2 whole, which is shorter than its diff:
```python
import math

import jax
import jax.numpy as jnp
from jax import lax
from jax.experimental import pallas as pl
from jax.experimental.pallas import tpu as pltpu
from jax.sharding import Mesh, PartitionSpec as P

QUERY_HEADS = 32
KEY_VALUE_HEADS = 4
HEAD_SIZE = 128
SUFFIX_SLOTS = 128
CAP = 8
PLANE = ("x", "y")
SWAP = ((0, 1), (1, 0))
TAIL = 16
FACTOR = 1.0 / math.sqrt(HEAD_SIZE)
LOG2E = 1.0 / math.log(2.0)
BIG = 28 * 1024 * 1024
MOST = 58 * 1024 * 1024
F32, BF16 = jnp.float32, jnp.bfloat16


def iota(shape, dim):
    return lax.broadcasted_iota(jnp.int32, shape, dim)


def matmul(a, b, ca=1, cb=0):
    return lax.dot_general(a, b, (((ca,), (cb,)), ((), ())), preferred_element_type=F32)


def high_part(value):
    return value.astype(BF16).astype(F32)


def whole_spec(shape):
    return pl.BlockSpec(shape, lambda *_: (0,) * len(shape))


HBM = pl.BlockSpec(memory_space=pltpu.HBM)
SMEM = pl.BlockSpec(memory_space=pltpu.SMEM)
VMEM = pl.BlockSpec(memory_space=pltpu.VMEM)
PIECES = 4


def layout_of(length, chips, feats, wide, suffix_rows):
    weights = 2 * length
    skeys = weights + chips * feats // 2
    svalues = skeys + suffix_rows
    lengths = svalues + suffix_rows
    return 0, length, weights, skeys, svalues, lengths, lengths + TAIL


def pack_kernel(
    core_ref,
    len_ref,
    prompt_ref,
    query_ref,
    k_ref,
    v_ref,
    sk_ref,
    sv_ref,
    w_ref,
    packed_ref,
    place_ref,
    tails_ref,
    bundle_ref,
    stage_ref,
    in_sems,
    out_sems,
):
    length, wide = k_ref.shape
    feats, chips = w_ref.shape[0], tails_ref.shape[0] // TAIL
    width = w_ref.shape[1] // (2 * chips)
    spots = layout_of(length, chips, feats, wide, sk_ref.shape[0])
    moves = []

    def move(source, rows, columns):
        copy = pltpu.make_async_copy(
            source, stage_ref.at[rows, columns], in_sems.at[len(moves)]
        )
        copy.start()
        moves.append((copy, rows, columns))

    piece = length // PIECES
    every = pl.ds(0, wide)
    for ref, first in ((k_ref, spots[0]), (v_ref, spots[1])):
        for i in range(PIECES):
            move(ref.at[pl.ds(i * piece, piece), :], pl.ds(first + i * piece, piece), every)
    other = 1 - core_ref[0]
    for k in range(chips):
        columns = pl.ds(pl.multiple_of(2 * width * k + other * width, width), width)
        rows = pl.ds(spots[2] + (k // 2) * feats, feats)
        move(w_ref.at[:, columns], rows, pl.ds((k % 2) * width, width))
    for ref, first in ((sk_ref, spots[3]), (sv_ref, spots[4])):
        move(ref, pl.ds(first, ref.shape[0]), every)
    line = iota((TAIL, wide), 0)
    lengths = jnp.where(line == 0, len_ref[0], jnp.where(line == 1, len_ref[1], 0))
    stage_ref[spots[5] :, :] = lengths.astype(F32).astype(BF16)

    prompt = prompt_ref[...]
    slots, rows = place_ref.shape
    lines = iota((slots, rows), 0)
    named = (lines == prompt).astype(F32)
    earlier = (iota((rows, rows), 0) < iota((rows, rows), 1)).astype(F32)
    before = matmul(named.astype(BF16), earlier.astype(BF16))
    rank = jnp.sum(before * named, axis=0, keepdims=True).astype(jnp.int32)
    place = (lines == prompt * CAP + rank).astype(F32).astype(BF16)
    place_ref[...] = place
    query = query_ref[...]
    packed_ref[...] = matmul(place, query).astype(BF16)

    line, row = iota((chips * TAIL, rows), 0), iota((chips * TAIL, rows), 1)
    spot = line & 7
    asks = (spot < 4) & (row == (line >> 4) * 4 + spot)
    tails_ref[...] = matmul(asks.astype(F32).astype(BF16), query).astype(BF16)

    leaving = []

    def leave(rows, columns):
        copy = pltpu.make_async_copy(
            stage_ref.at[rows, columns], bundle_ref.at[rows, columns], out_sems.at[len(leaving)]
        )
        copy.start()
        leaving.append(copy)

    leave(pl.ds(spots[5], TAIL), every)
    for copy, rows, columns in moves:
        copy.wait()
        leave(rows, columns)
    for copy in leaving:
        copy.wait()


def pack(core, lengths, prompt, queries, keys, values, skeys, svalues, w, slots, chips):
    rows = queries.shape[0]
    length, wide = keys.shape
    height = layout_of(length, chips, w.shape[0], wide, skeys.shape[0])[-1]
    return pl.pallas_call(
        pack_kernel,
        in_specs=[SMEM, SMEM, VMEM, VMEM] + [HBM] * 5,
        out_specs=(VMEM, VMEM, VMEM, HBM),
        out_shape=(
            jax.ShapeDtypeStruct((slots, HEAD_SIZE), BF16),
            jax.ShapeDtypeStruct((slots, rows), BF16),
            jax.ShapeDtypeStruct((chips * TAIL, HEAD_SIZE), BF16),
            jax.ShapeDtypeStruct((height, wide), BF16),
        ),
        scratch_shapes=[
            pltpu.VMEM((height, wide), BF16),
            pltpu.SemaphoreType.DMA((2 * PIECES + chips + 2,)),
            pltpu.SemaphoreType.DMA((2 * PIECES + chips + 3,)),
        ],
        compiler_params=pltpu.CompilerParams(vmem_limit_bytes=MOST),
        name="pack",
    )(core, lengths, prompt, queries, keys, values, skeys, svalues, w)


def spread_kernel(arrived_ref, tails_ref, out_ref):
    chips, height, _ = out_ref.shape
    arrived = arrived_ref[...]
    for k in range(chips):
        out_ref[k, : height - TAIL, :] = arrived
        out_ref[k, height - TAIL :, :] = tails_ref[k * TAIL : (k + 1) * TAIL]


def spread(arrived, tails, chips):
    return pl.pallas_call(
        spread_kernel,
        out_shape=jax.ShapeDtypeStruct((chips, arrived.shape[0] + TAIL, HEAD_SIZE), BF16),
        compiler_params=pltpu.CompilerParams(vmem_limit_bytes=BIG),
        name="spread",
    )(arrived, tails)


def suffix_part(core, lengths, query, keys, values):
    rows, span = query.shape[0], keys.shape[0]
    scores = matmul(query, keys, 1, 1)
    column = iota((rows, span), 1)
    block, place = column >> 7, column & 127
    live = ((iota((rows, span), 0) & 7) == ((block + 2 * core) & 3)) & (place < lengths)
    peak = jnp.max(jnp.where(live, scores, -1e30), axis=1, keepdims=True)
    shift = high_part(peak * FACTOR)
    weights = jnp.where(live, jnp.exp2(scores * (FACTOR * LOG2E) - shift * LOG2E), 0.0)
    ones = jnp.ones((span, HEAD_SIZE), BF16)
    outs = matmul(weights.astype(BF16), jnp.concatenate([values, ones], axis=1))
    lane = iota((rows, HEAD_SIZE), 1)
    total = outs[:, HEAD_SIZE:]
    total_high = high_part(total)
    numbers = jnp.where(
        lane == 0,
        shift,
        jnp.where(lane == 1, total_high, jnp.where(lane == 2, total - total_high, 0.0)),
    )
    line = iota((rows, HEAD_SIZE), 0) & (TAIL - 1)
    return jnp.where(
        line < 4, outs[:, :HEAD_SIZE], jnp.where((line >= 8) & (line < 12), numbers, 0.0)
    )


def attend_kernel(
    core_ref,
    len_ref,
    here_ref,
    k_ref,
    v_ref,
    sk_ref,
    sv_ref,
    bundle_ref,
    out_ref,
    w_ref,
    k_buf,
    v_buf,
    sk_buf,
    sv_buf,
    len_buf,
    even_ref,
    odd_ref,
    sems,
):
    step = pl.program_id(0)
    steps = k_buf.shape[0]
    total_heads = here_ref.shape[0]
    slots = here_ref.shape[1] - TAIL
    length, wide = k_ref.shape
    chips = total_heads * steps
    own_suffix = sk_ref.shape[0]
    spots = layout_of(length, chips, HEAD_SIZE, wide, own_suffix)
    part = wide // steps
    kv_heads = part // HEAD_SIZE
    heads = total_heads // kv_heads
    parts = (
        (k_ref, spots[0], length, k_buf),
        (v_ref, spots[1], length, v_buf),
        (sk_ref, spots[3], own_suffix, sk_buf),
        (sv_ref, spots[4], own_suffix, sv_buf),
    )

    def copies(i, s):
        ref, first, count, buf = parts[i]
        columns = pl.ds(pl.multiple_of(s * part, part), part)
        return (
            pltpu.make_async_copy(
                ref.at[:, columns], buf.at[s, pl.ds(0, count)], sems.at[s, 2 * i]
            ),
            pltpu.make_async_copy(
                bundle_ref.at[pl.ds(first, count), columns],
                buf.at[s, pl.ds(count, count)],
                sems.at[s, 2 * i + 1],
            ),
        )

    len_copy = pltpu.make_async_copy(
        bundle_ref.at[pl.ds(spots[5], TAIL), :], len_buf, sems.at[0, 2 * len(parts)]
    )

    w_copy = pltpu.make_async_copy(
        bundle_ref.at[pl.ds(spots[2], w_ref.shape[0]), :], w_ref, sems.at[1, 2 * len(parts)]
    )

    @pl.when(step == 0)
    def _():
        for s in range(steps):
            for i in (0, 2, 3, 1):
                for copy in copies(i, s):
                    copy.start()
            if s == 0:
                len_copy.start()
        w_copy.start()
        len_copy.wait()

    def arrive(i):
        for copy in copies(i, step):
            copy.wait()

    cuts = [slice(j * HEAD_SIZE, (j + 1) * HEAD_SIZE) for j in range(kv_heads)]
    ones = jnp.ones((2 * length, HEAD_SIZE), BF16)
    held = (even_ref, odd_ref)
    units = [(j, j * heads + 2 * p) for j in range(kv_heads) for p in range(heads // 2)]

    def scores(unit):
        j, first = units[unit]
        query = jnp.concatenate([here_ref[first + i, :slots, :] for i in range(2)], axis=0)
        value = matmul(query, k_buf[step, :, cuts[j]], 1, 1)
        held[unit % 2][...] = value
        return jnp.max(value, axis=1, keepdims=True)

    arrive(0)
    peak = scores(0)
    arrive(2)
    arrive(3)
    span = 2 * own_suffix
    block = iota((1, span), 1) >> 7
    others = len_buf[...].astype(F32)
    pick = lambda row: others[row : row + 1, :HEAD_SIZE].astype(jnp.int32)
    fixed = lambda row: jnp.full((1, HEAD_SIZE), len_ref[row], jnp.int32)
    lengths = jnp.concatenate([fixed(0), fixed(1), pick(0), pick(1)], axis=1)
    tails = []
    for j in range(kv_heads):
        asks = jnp.concatenate([here_ref[j * heads + h, slots:, :] for h in range(heads)], axis=0)
        tails.append(
            suffix_part(
                core_ref[0], lengths, asks, sk_buf[step, :, cuts[j]], sv_buf[step, :, cuts[j]]
            )
        )
    arrive(1)

    lane = iota((2 * slots, HEAD_SIZE), 1)
    for unit, (j, start) in enumerate(units):
        peak_next = scores(unit + 1) if unit + 1 < len(units) else None
        shift = high_part(peak * FACTOR)
        weights = jnp.exp2(held[unit % 2][...] * (FACTOR * LOG2E) - shift * LOG2E).astype(BF16)
        outs = matmul(weights, jnp.concatenate([v_buf[step, :, cuts[j]], ones], axis=1))
        total = outs[:, HEAD_SIZE:]
        total_high = high_part(total)
        numbers = jnp.where(
            lane == 4,
            shift,
            jnp.where(lane == 5, total_high, jnp.where(lane == 6, total - total_high, 0.0)),
        )
        for i in range(2):
            h = start + i
            cut = slice(i * slots, (i + 1) * slots)
            out_ref[h, :slots, :] = outs[cut, :HEAD_SIZE].astype(BF16)
            place = (h - j * heads) * TAIL
            tail = tails[j][place : place + TAIL] + numbers[cut].T[:TAIL]
            out_ref[h, slots:, :] = tail.astype(BF16)
        peak = peak_next

    @pl.when(step == steps - 1)
    def _():
        w_copy.wait()


def attend(core, lengths, here, keys, values, skeys, svalues, bundle):
    chips, height, _ = here.shape
    steps = 2
    heads = chips // steps
    length, wide = keys.shape
    part = wide // steps
    slots, own_suffix = height - TAIL, skeys.shape[0]
    chunk = pl.BlockSpec((heads, height, HEAD_SIZE), lambda j: (j, 0, 0))
    return pl.pallas_call(
        attend_kernel,
        grid=(steps,),
        in_specs=[SMEM, SMEM, chunk] + [HBM] * 5,
        out_specs=(chunk, whole_spec((chips * HEAD_SIZE // 2, wide))),
        out_shape=(
            jax.ShapeDtypeStruct(here.shape, BF16),
            jax.ShapeDtypeStruct((chips * HEAD_SIZE // 2, wide), BF16),
        ),
        scratch_shapes=[
            pltpu.VMEM((steps, 2 * length, part), BF16),
            pltpu.VMEM((steps, 2 * length, part), BF16),
            pltpu.VMEM((steps, 2 * own_suffix, part), BF16),
            pltpu.VMEM((steps, 2 * own_suffix, part), BF16),
            pltpu.VMEM((TAIL, wide), BF16),
            pltpu.VMEM((2 * slots, 2 * length), F32),
            pltpu.VMEM((2 * slots, 2 * length), F32),
            pltpu.SemaphoreType.DMA((steps, 9)),
        ],
        compiler_params=pltpu.CompilerParams(vmem_limit_bytes=36 * 1024 * 1024),
        cost_estimate=pl.CostEstimate(
            flops=8 * chips * height * length * HEAD_SIZE,
            bytes_accessed=10 * length * wide,
            transcendentals=2 * chips * height * length,
        ),
        name="attend",
    )(core, lengths, here, keys, values, skeys, svalues, bundle)


def merge_kernel(own_ref, sent_ref):
    chips, height, _ = own_ref.shape
    slots, groups = height - TAIL, sent_ref.shape[0]
    tails = own_ref[:, slots:, :].astype(F32)
    shift = tails[:, 4, :]
    total = tails[:, 5, :] + tails[:, 6, :]
    top = jnp.max(shift, axis=0, keepdims=True)
    scale = jnp.exp(shift - top)
    whole = jnp.sum(total * scale, axis=0, keepdims=True)
    whole_high = high_part(whole)
    line = iota((8, slots), 0)
    numbers = jnp.where(
        line == 0, top, jnp.where(line == 1, whole_high, jnp.where(line == 2, whole - whole_high, 0.0))
    )
    rest = jnp.zeros((HEAD_SIZE - chips - 8, slots), F32)
    across = jnp.concatenate([scale / whole, numbers, rest], axis=0).T
    mean = jnp.zeros((slots, HEAD_SIZE), F32)
    for k in range(chips):
        mean += across[:, k : k + 1] * own_ref[k, :slots, :].astype(F32)
    cap = slots // groups
    both = [value.reshape(groups, cap, HEAD_SIZE) for value in (mean, across)]
    sent_ref[...] = jnp.concatenate(both, axis=1).astype(BF16)


def merge(own, groups):
    chips, height, _ = own.shape
    cap = (height - TAIL) // groups
    return pl.pallas_call(
        merge_kernel,
        out_shape=jax.ShapeDtypeStruct((groups, 2 * cap, HEAD_SIZE), BF16),
        compiler_params=pltpu.CompilerParams(vmem_limit_bytes=BIG),
        name="merge",
    )(own)


def finish_kernel(place_ref, back_ref, tails_ref, out_ref):
    groups, double, _ = back_ref.shape
    cap, rows = double // 2, place_ref.shape[1]
    chips = tails_ref.shape[0]
    span = chips * TAIL
    back = back_ref[...].astype(F32)
    means = back[:, :cap].reshape(groups * cap, HEAD_SIZE).astype(BF16)
    numbers = back[:, cap:].reshape(groups * cap, HEAD_SIZE).astype(BF16)
    both = matmul(place_ref[...], jnp.concatenate([means, numbers], axis=1), 0, 0)
    pre_mean, pre_numbers = both[:, :HEAD_SIZE], both[:, HEAD_SIZE:]
    pre_top = pre_numbers[:, chips : chips + 1]
    pre_total = pre_numbers[:, chips + 1 : chips + 2] + pre_numbers[:, chips + 2 : chips + 3]

    tails = tails_ref[...].reshape(span, HEAD_SIZE)
    line, column = iota((2 * rows, span), 0), iota((2 * rows, span), 1)
    row = line & (rows - 1)
    spot = (row >> 2) * TAIL + (row & 3) + jnp.where(line < rows, 0, 8)
    picked = matmul((column == spot).astype(F32).astype(BF16), tails)
    suf_out, suf_numbers = picked[:rows], picked[rows:]
    suf_top = suf_numbers[:, 0:1]
    suf_total = suf_numbers[:, 1:2] + suf_numbers[:, 2:3]

    peak = jnp.maximum(pre_top, suf_top)
    left = jnp.exp(pre_top - peak) * pre_total
    right = jnp.exp(suf_top - peak)
    attended = (pre_mean * left + suf_out * right) / (left + suf_total * right)
    out_ref[...] = attended.astype(BF16)


def finish(place, back, own):
    chips, height, _ = own.shape
    rows = place.shape[1]
    return pl.pallas_call(
        finish_kernel,
        grid=(1,),
        in_specs=[
            whole_spec(place.shape),
            whole_spec(back.shape),
            pl.BlockSpec((chips, TAIL, HEAD_SIZE), lambda i: (0, height // TAIL - 1, 0)),
        ],
        out_specs=whole_spec((rows, HEAD_SIZE)),
        out_shape=jax.ShapeDtypeStruct((rows, HEAD_SIZE), BF16),
        name="finish",
    )(place, back, own)


def project_kernel(core_ref, a_ref, w0_ref, w1_ref, out_ref):
    width = out_ref.shape[2]
    feats = w0_ref.shape[0]
    core = core_ref[0]
    attended = jnp.concatenate([a_ref[core], a_ref[1 - core]], axis=1)
    for k in range(out_ref.shape[0]):
        own = w0_ref[:, pl.ds(pl.multiple_of(2 * width * k + core * width, width), width)]
        half, side = (k // 2) * feats, (k % 2) * width
        other = w1_ref[half : half + feats, side : side + width]
        out_ref[k] = matmul(attended, jnp.concatenate([own, other], axis=0)).astype(BF16)


def project(core, attended, w, w_other, chips):
    _, rows, feats = attended.shape
    width = w.shape[1] // (2 * chips)
    steps = 2
    part = chips // steps
    high = part * feats // 2
    return pl.pallas_call(
        project_kernel,
        grid=(steps,),
        in_specs=[
            SMEM,
            whole_spec(attended.shape),
            pl.BlockSpec((feats, 2 * width * part), lambda i: (0, i)),
            pl.BlockSpec((high, 2 * width), lambda i: (i, 0)),
        ],
        out_specs=pl.BlockSpec((part, rows, width), lambda i: (i, 0, 0)),
        out_shape=jax.ShapeDtypeStruct((chips, rows, width), BF16),
        compiler_params=pltpu.CompilerParams(vmem_limit_bytes=BIG),
        name="project",
    )(core, attended, w, w_other)


def body(
    queries,
    row_prompt,
    prompt_prefix_keys,
    prompt_prefix_values,
    row_suffix_keys,
    row_suffix_values,
    suffix_lengths,
    w_out,
):
    groups = lax.axis_size("grp")
    chips = lax.axis_size("x") * lax.axis_size("y")
    core = lax.axis_index("core").reshape(1).astype(jnp.int32)
    row_grp = queries.shape[0]
    slots = groups * CAP
    keys, values = prompt_prefix_keys[0], prompt_prefix_values[0]
    skeys = row_suffix_keys.reshape(-1, row_suffix_keys.shape[2])
    svalues = row_suffix_values.reshape(-1, row_suffix_values.shape[2])

    packed, place, tails, bundle = pack(
        core,
        suffix_lengths,
        row_prompt.reshape(1, row_grp),
        queries,
        keys,
        values,
        skeys,
        svalues,
        w_out,
        slots,
        chips,
    )
    bundle = lax.ppermute(bundle, "core", SWAP)
    arrived = lax.all_to_all(packed, "grp", split_axis=0, concat_axis=0, tiled=True)

    here = lax.all_to_all(
        spread(arrived, tails, chips), PLANE, split_axis=0, concat_axis=0, tiled=True
    )
    parts, w_other = attend(core, suffix_lengths, here, keys, values, skeys, svalues, bundle)
    own = lax.all_to_all(parts, PLANE, split_axis=0, concat_axis=0, tiled=True)

    sent = merge(own, groups)
    back = lax.all_to_all(sent, "grp", split_axis=0, concat_axis=0, tiled=True)
    attended = lax.all_gather(finish(place, back, own), "core", axis=0, tiled=False)
    shares = project(core, attended, w_out, w_other, chips)
    shares = lax.all_to_all(shares, PLANE, split_axis=0, concat_axis=0, tiled=True)
    return jnp.sum(shares.astype(F32), axis=0).astype(BF16)


def solution(mesh):
    side = math.isqrt(mesh.shape["seq"] // 2)
    fine = Mesh(
        mesh.devices.reshape(mesh.shape["grp"], side, side, 2), ("grp", "x", "y", "core")
    )
    seq = ("x", "y", "core")
    every = ("grp",) + seq
    in_specs = (
        P("grp", seq),
        P("grp", None),
        P("grp", seq, None),
        P("grp", seq, None),
        P(every, None, None),
        P(every, None, None),
        P(every),
        P(seq, None),
    )
    return jax.shard_map(
        body, mesh=fine, in_specs=in_specs, out_specs=P("grp", seq), check_vma=False
    )
```

time: 128 us -> 116 us (0.906)
  starting transfers between devices: 32.5 us -> 8.77 us
  blocking collectives: 67.4 us -> 85.6 us
  local copies, waits for them, and re-layouts: 6.5 us -> 3.06 us
  waiting for transfers between devices: 2.47 us -> 0.01 us
    ppermute x7 -> x1, starting transfers between devices: 25.7 us -> 8.77 us  [body(): bundle = lax.ppermute(bundle, 'core', SWAP)]
    all_to_all x0 -> x1, blocking collectives: none -> 16.9 us  [body(): lax.all_to_all(spread(arrived, tails, chips), PLANE, split_axis=0, concat...]
    all_to_all x1 -> x0, starting transfers between devices: 6.75 us -> none  [body(): lax.all_to_all(spread, PLANE, split_axis=0, concat_axis=0, tiled=True)]
    all_gather x0 -> x1, blocking collectives: none -> 6.67 us  [body(): lax.all_gather(finish(place, back, own), 'core', axis=0, tiled=False)]
    all_to_all x1, blocking collectives: 18.2 us -> 12.7 us  [body(): own = lax.all_to_all(parts, PLANE, split_axis=0, concat_axis=0, tiled=True)]
    concatenate x1 -> x0, local copies, waits for them, and re-layouts: 4.14 us -> none  [body(): jnp.concatenate([jnp.broadcast_to(arrived[None], (chips, slots, HEAD_SIZE...]
    ppermute x7 -> x1, waiting for transfers between devices: 2.3 us -> 0.01 us  [body(): bundle = lax.ppermute(bundle, 'core', SWAP)]
    unnamed x17 -> x20, local copies, waits for them, and re-layouts: 2.26 us -> 3.06 us
  transfers between devices with their start and end apart: 8 -> 1, of which waited for: 3 -> 0; matrix products, arithmetic and copies ran while one was open for 3% -> 0% of each run, Pallas kernels for 10% -> 0%
where the time goes in v2:
time: 116 us; the launch traced here: 115 us
  blocking collectives  85.6 us (74%)
  Pallas kernels  17.2 us (15%)
  starting transfers between devices  8.77 us (8%)
  local copies, waits for them, and re-layouts  3.06 us (3%)
    all_to_all x1, blocking collectives, body(): lax.all_to_all(packed, 'grp', split_axis=0, concat_axis=0, tiled=True)  21 us
    all_to_all x1, blocking collectives, body(): lax.all_to_all(spread(arrived, tails, chips), PLANE, split_axis=0, concat...  16.9 us
    all_to_all x1, blocking collectives, body(): back = lax.all_to_all(sent, 'grp', split_axis=0, concat_axis=0, tiled=True)  14.9 us
    all_to_all x1, blocking collectives, body(): lax.all_to_all(shares, PLANE, split_axis=0, concat_axis=0, tiled=True)  13.4 us
    all_to_all x1, blocking collectives, body(): own = lax.all_to_all(parts, PLANE, split_axis=0, concat_axis=0, tiled=True)  12.7 us
    ppermute x1, starting transfers between devices, body(): bundle = lax.ppermute(bundle, 'core', SWAP)  8.77 us
    pallas_call x1, Pallas kernels, attend(): pl.pallas_call(attend_kernel, grid=(steps,), in_specs=[SMEM, SMEM, chunk]...  8.44 us
    all_gather x1, blocking collectives, body(): lax.all_gather(finish(place, back, own), 'core', axis=0, tiled=False)  6.67 us
  transfers between devices with their start and end apart: 1, of which 0 were waited for; matrix products, arithmetic and copies ran while one was open for 0% of the time, Pallas kernels for 0%

profile of v2, /device:TPU:1, one launch (start us, length us, event | category | flops | bytes accessed | tf_op | source)
XLA Modules:
  0.0 115.4 jit_solution(3509262589895399156)
XLA Ops:
  0.0 0.0 copy-start.9
  0.0 0.0 copy-start.6
  0.0 0.0 copy-start.2
  0.0 0.0 copy-start.3
  0.0 0.0 copy-start.7
  0.0 5.3 %pack.1 = (bf16[128,128]{1,0:T(8,128)(2,1)}, bf16[128,64]{1,0:T(8,128)(2,1)}, bf16[256,128]{1,0:T(8,128)(2,1)}, bf16[3600,512]{1,0:T(8,128)(2,1)}) custom-call(s32[1]{0:T(128)} %bitcast.core_ref, s32[2]{0:T(128)} %len_ref.3, s32[1,64]{1,0:T(1,128)} %bitcast.20, bf16[64,128]{1,0:T(8,128)(2,1)} %query_ref.1, bf16[1024,512]{1,0:T(8,128)(2,1)} %bitcast.9, ...), custom_call_target="tpu_custom_call" | custom-call | tf_op jit(solution)/shard_map/pack/pallas_call | solution.py:140
  5.3 8.8 %collective-permute-start = (bf16[3600,512]{1,0:T(8,128)(2,1)}, bf16[3600,512]{1,0:T(8,128)(2,1)S(1)}, u32[]{:S(2)}, u32[]{:S(2)}) collective-permute-start(bf16[3600,512]{1,0:T(8,128)(2,1)} %get-tuple-element.14), channel_id=1, source_target_pairs={{0,1},{1,0},{2,3},{3,2},{4,5},{5,4},{6,7},{7,6},{8,9},{9,8},{10,11... | collective-permute-start | bytes 11059208 | tf_op jit(solution)/shard_map/ppermute | solution.py:520
  14.1 21.0 %all_to_all.31 = bf16[16,8,128]{2,1,0:T(8,128)(2,1)S(1)} all-to-all(bf16[16,8,128]{2,1,0:T(8,128)(2,1)} %bitcast.19), channel_id=1, replica_groups=mesh['grp'=16,'x'=4,'y'=4,'core'=2] {'grp'}, dimensions={0} | all-to-all | bytes 65536 | tf_op jit(solution)/shard_map/all_to_all | solution.py:521
  35.2 0.0 copy-start.8
  35.2 0.8 copy-done.8
  36.0 0.1 spread.1
  36.1 16.9 %all_to_all.32.here_ref = bf16[16,144,128]{2,1,0:T(8,128)(2,1)S(1)} all-to-all(bf16[16,144,128]{2,1,0:T(8,128)(2,1)S(1)} %spread.1), channel_id=1, replica_groups=mesh['grp'=16,'x'=4,'y'=4,'core'=2] {'x','y'}, dimensions={0} | all-to-all | bytes 1179648 | tf_op jit(solution)/shard_map/all_to_all | solution.py:523
  53.0 0.0 copy-start
  53.0 0.0 collective-permute-done.bundle_ref
  53.0 0.0 copy-done.9
  53.0 0.0 copy-done.6
  53.0 0.0 copy-done.2
  53.0 0.0 copy-done.3
  53.0 0.0 copy-done.7
  53.0 8.4 %attend.1 = (bf16[16,144,128]{2,1,0:T(8,128)(2,1)S(1)}, bf16[1024,512]{1,0:T(8,128)(2,1)S(1)}) custom-call(s32[1]{0:T(128)} %bitcast.core_ref, s32[2]{0:T(128)S(1)} %copy-done.9, bf16[16,144,128]{2,1,0:T(8,128)(2,1)S(1)} %all_to_all.32.here_ref, bf16[1024,512]{1,0:T(8,128)(2,1)S(1)} %bitcast.10, bf16[1024,512]{1,0:T(8,128)(2,1)S(1)} %bitcast.12, ...), custom_call_target="tpu_custom_call" | custom-call | flops 2415919104 | bytes 5242880 | tf_op jit(solution)/shard_map/attend/pallas_call | solution.py:344
  61.5 0.0 copy-start.4
  61.5 1.0 copy-done.4
  62.4 12.7 %all_to_all.33.own_ref.tails_ref = bf16[16,144,128]{2,1,0:T(8,128)(2,1)S(1)} all-to-all(bf16[16,144,128]{2,1,0:T(8,128)(2,1)S(1)} %get-tuple-element.15), channel_id=1, replica_groups=mesh['grp'=16,'x'=4,'y'=4,'core'=2] {'x','y'}, dimensions={0} | all-to-all | bytes 1179648 | tf_op jit(solution)/shard_map/all_to_all | solution.py:527
  75.1 0.0 copy-start.1
  75.1 0.5 merge.1
  75.7 14.9 %all_to_all.34.back_ref = bf16[16,16,128]{2,1,0:T(8,128)(2,1)} all-to-all(bf16[16,16,128]{2,1,0:T(8,128)(2,1)S(1)} %merge.1), channel_id=1, replica_groups=mesh['grp'=16,'x'=4,'y'=4,'core'=2] {'grp'}, dimensions={0} | all-to-all | bytes 131072 | tf_op jit(solution)/shard_map/all_to_all | solution.py:530
  90.6 0.0 copy-done.1
  90.6 2.0 %finish.1 = bf16[64,128]{1,0:T(8,128)(2,1)} custom-call(bf16[128,64]{1,0:T(8,128)(2,1)} %get-tuple-element.11.place_ref, bf16[16,16,128]{2,1,0:T(8,128)(2,1)} %all_to_all.34.back_ref, bf16[16,144,128]{2,1,0:T(8,128)(2,1)} %copy-done.1), custom_call_target="tpu_custom_call" | custom-call | tf_op jit(solution)/shard_map/finish/pallas_call | solution.py:440
  92.6 6.7 %all-gather = bf16[128,128]{1,0:T(8,128)(2,1)S(1)} all-gather(bf16[64,128]{1,0:T(8,128)(2,1)} %finish.1), channel_id=2, replica_groups=mesh['grp'=16,'x'=4,'y'=4,'core'=2] {'core'}, dimensions={0}, use_global_device_ids=true | all-gather | bytes 49152 | tf_op jit(solution)/shard_map/all_gather | solution.py:531
  99.2 0.0 copy-done
  99.3 0.0 copy-start.5
  99.3 1.2 %copy-done.5 = bf16[1024,512]{1,0:T(8,128)(2,1)S(1)} copy-done((bf16[1024,512]{1,0:T(8,128)(2,1)S(1)}, bf16[1024,512]{1,0:T(8,128)(2,1)}, u32[]{:S(2)}) %copy-start.5) | copy-done | bytes 1048600
  100.5 0.8 project.1
  101.3 13.4 %all_to_all.35 = bf16[16,64,256]{2,1,0:T(8,128)(2,1)S(1)} all-to-all(bf16[16,64,256]{2,1,0:T(8,128)(2,1)S(1)} %project.1), channel_id=1, replica_groups=mesh['grp'=16,'x'=4,'y'=4,'core'=2] {'x','y'}, dimensions={0} | all-to-all | bytes 1048576 | tf_op jit(solution)/shard_map/all_to_all | solution.py:533
  114.7 0.7 reduce_sum.12
Async XLA Ops:
  0.0 53.0 %copy-start.9 = (s32[2]{0:T(128)S(1)}, s32[2]{0:T(128)}, u32[]{:S(2)}) copy-start(s32[2]{0:T(128)} %len_ref.3) | copy-start | bytes 28
  0.0 53.0 %copy-start.6 = (bf16[2,128,512]{2,1,0:T(8,128)(2,1)S(1)}, bf16[2,128,512]{2,1,0:T(8,128)(2,1)}, u32[]{:S(2)}) copy-start(bf16[2,128,512]{2,1,0:T(8,128)(2,1)} %param.12) | copy-start | bytes 786436
  0.0 53.0 %copy-start.2 = (bf16[1,1024,512]{2,1,0:T(8,128)(2,1)S(1)}, bf16[1,1024,512]{2,1,0:T(8,128)(2,1)}, u32[]{:S(2)}) copy-start(bf16[1,1024,512]{2,1,0:T(8,128)(2,1)} %param.10) | copy-start | bytes 3145732
  0.0 53.0 %copy-start.3 = (bf16[1,1024,512]{2,1,0:T(8,128)(2,1)S(1)}, bf16[1,1024,512]{2,1,0:T(8,128)(2,1)}, u32[]{:S(2)}) copy-start(bf16[1,1024,512]{2,1,0:T(8,128)(2,1)} %param.11) | copy-start | bytes 3145732
  0.0 53.0 %copy-start.7 = (bf16[2,128,512]{2,1,0:T(8,128)(2,1)S(1)}, bf16[2,128,512]{2,1,0:T(8,128)(2,1)}, u32[]{:S(2)}) copy-start(bf16[2,128,512]{2,1,0:T(8,128)(2,1)} %param.13) | copy-start | bytes 786436
  5.3 47.6 %collective-permute-start = (bf16[3600,512]{1,0:T(8,128)(2,1)}, bf16[3600,512]{1,0:T(8,128)(2,1)S(1)}, u32[]{:S(2)}, u32[]{:S(2)}) collective-permute-start(bf16[3600,512]{1,0:T(8,128)(2,1)} %get-tuple-element.14), channel_id=1, source_target_pairs={{0,1},{1,0},{2,3},{3,2},{4,5},{5,4},{6,7},{7,6},{8,9},{9,8},{10,11... | collective-permute-start | bytes 11059208 | tf_op jit(solution)/shard_map/ppermute | solution.py:520
  35.2 0.8 copy-start.8
  53.0 46.3 %copy-start = (bf16[128,8192]{1,0:T(8,128)(2,1)S(1)}, bf16[128,8192]{1,0:T(8,128)(2,1)}, u32[]{:S(2)}) copy-start(bf16[128,8192]{1,0:T(8,128)(2,1)} %w0_ref.1) | copy-start | bytes 6291460
  61.5 1.0 copy-start.4
  75.1 15.4 %copy-start.1 = (bf16[16,144,128]{2,1,0:T(8,128)(2,1)}, bf16[16,144,128]{2,1,0:T(8,128)(2,1)S(1)}, u32[]{:S(2)}) copy-start(bf16[16,144,128]{2,1,0:T(8,128)(2,1)S(1)} %all_to_all.33.own_ref.tails_ref) | copy-start | bytes 1769476
  99.3 1.2 %copy-start.5 = (bf16[1024,512]{1,0:T(8,128)(2,1)S(1)}, bf16[1024,512]{1,0:T(8,128)(2,1)}, u32[]{:S(2)}) copy-start(bf16[1024,512]{1,0:T(8,128)(2,1)} %copy-done.4) | copy-start | bytes 3145732

commit v3 on v2

--- a/solution.py
+++ b/solution.py
@@ -52,27 +52,57 @@
     return 0, length, weights, skeys, svalues, lengths, lengths + TAIL
 
 
-def pack_kernel(
+def pack_kernel(prompt_ref, query_ref, packed_ref, place_ref, tails_ref):
+    prompt = prompt_ref[...]
+    slots, rows = place_ref.shape
+    chips = tails_ref.shape[0] // TAIL
+    lines = iota((slots, rows), 0)
+    named = (lines == prompt).astype(F32)
+    earlier = (iota((rows, rows), 0) < iota((rows, rows), 1)).astype(F32)
+    before = matmul(named.astype(BF16), earlier.astype(BF16))
+    rank = jnp.sum(before * named, axis=0, keepdims=True).astype(jnp.int32)
+    place = (lines == prompt * CAP + rank).astype(F32).astype(BF16)
+    place_ref[...] = place
+    query = query_ref[...]
+    packed_ref[...] = matmul(place, query).astype(BF16)
+
+    line, row = iota((chips * TAIL, rows), 0), iota((chips * TAIL, rows), 1)
+    spot = line & 7
+    asks = (spot < 4) & (row == (line >> 4) * 4 + spot)
+    tails_ref[...] = matmul(asks.astype(F32).astype(BF16), query).astype(BF16)
+
+
+def pack(prompt, queries, slots, chips):
+    rows = queries.shape[0]
+    return pl.pallas_call(
+        pack_kernel,
+        out_shape=(
+            jax.ShapeDtypeStruct((slots, HEAD_SIZE), BF16),
+            jax.ShapeDtypeStruct((slots, rows), BF16),
+            jax.ShapeDtypeStruct((chips * TAIL, HEAD_SIZE), BF16),
+        ),
+        compiler_params=pltpu.CompilerParams(vmem_limit_bytes=BIG),
+        name="pack",
+    )(prompt, queries)
+
+
+def bundle_kernel(
     core_ref,
     len_ref,
-    prompt_ref,
-    query_ref,
     k_ref,
     v_ref,
     sk_ref,
     sv_ref,
     w_ref,
-    packed_ref,
-    place_ref,
-    tails_ref,
     bundle_ref,
     stage_ref,
     in_sems,
     out_sems,
 ):
     length, wide = k_ref.shape
-    feats, chips = w_ref.shape[0], tails_ref.shape[0] // TAIL
-    width = w_ref.shape[1] // (2 * chips)
+    feats = w_ref.shape[0]
+    chips = w_ref.shape[1] // wide
+    width = wide // 2
     spots = layout_of(length, chips, feats, wide, sk_ref.shape[0])
     moves = []
 
@@ -99,23 +129,6 @@
     lengths = jnp.where(line == 0, len_ref[0], jnp.where(line == 1, len_ref[1], 0))
     stage_ref[spots[5] :, :] = lengths.astype(F32).astype(BF16)
 
-    prompt = prompt_ref[...]
-    slots, rows = place_ref.shape
-    lines = iota((slots, rows), 0)
-    named = (lines == prompt).astype(F32)
-    earlier = (iota((rows, rows), 0) < iota((rows, rows), 1)).astype(F32)
-    before = matmul(named.astype(BF16), earlier.astype(BF16))
-    rank = jnp.sum(before * named, axis=0, keepdims=True).astype(jnp.int32)
-    place = (lines == prompt * CAP + rank).astype(F32).astype(BF16)
-    place_ref[...] = place
-    query = query_ref[...]
-    packed_ref[...] = matmul(place, query).astype(BF16)
-
-    line, row = iota((chips * TAIL, rows), 0), iota((chips * TAIL, rows), 1)
-    spot = line & 7
-    asks = (spot < 4) & (row == (line >> 4) * 4 + spot)
-    tails_ref[...] = matmul(asks.astype(F32).astype(BF16), query).astype(BF16)
-
     leaving = []
 
     def leave(rows, columns):
@@ -133,28 +146,44 @@
         copy.wait()
 
 
-def pack(core, lengths, prompt, queries, keys, values, skeys, svalues, w, slots, chips):
-    rows = queries.shape[0]
+def bundled(core, lengths, keys, values, skeys, svalues, w):
     length, wide = keys.shape
+    chips = w.shape[1] // wide
     height = layout_of(length, chips, w.shape[0], wide, skeys.shape[0])[-1]
     return pl.pallas_call(
-        pack_kernel,
-        in_specs=[SMEM, SMEM, VMEM, VMEM] + [HBM] * 5,
-        out_specs=(VMEM, VMEM, VMEM, HBM),
-        out_shape=(
-            jax.ShapeDtypeStruct((slots, HEAD_SIZE), BF16),
-            jax.ShapeDtypeStruct((slots, rows), BF16),
-            jax.ShapeDtypeStruct((chips * TAIL, HEAD_SIZE), BF16),
-            jax.ShapeDtypeStruct((height, wide), BF16),
-        ),
+        bundle_kernel,
+        in_specs=[SMEM, SMEM] + [HBM] * 5,
+        out_specs=HBM,
+        out_shape=jax.ShapeDtypeStruct((height, wide), BF16),
         scratch_shapes=[
             pltpu.VMEM((height, wide), BF16),
             pltpu.SemaphoreType.DMA((2 * PIECES + chips + 2,)),
             pltpu.SemaphoreType.DMA((2 * PIECES + chips + 3,)),
         ],
         compiler_params=pltpu.CompilerParams(vmem_limit_bytes=MOST),
-        name="pack",
-    )(core, lengths, prompt, queries, keys, values, skeys, svalues, w)
+        name="bundle",
+    )(core, lengths, keys, values, skeys, svalues, w)
+
+
+def asks_kernel(here_ref, asks_ref):
+    asks_ref[...] = here_ref[...]
+
+
+def asks_of(here):
+    chips, height, _ = here.shape
+    return pl.pallas_call(
+        asks_kernel,
+        grid=(1,),
+        in_specs=[
+            pl.BlockSpec((chips, TAIL, HEAD_SIZE), lambda i: (0, height // TAIL - 1, 0))
+        ],
+        out_specs=whole_spec((chips, TAIL, HEAD_SIZE)),
+        out_shape=jax.ShapeDtypeStruct((chips, TAIL, HEAD_SIZE), BF16),
+        cost_estimate=pl.CostEstimate(
+            flops=20_000_000_000, bytes_accessed=1 << 20, transcendentals=0
+        ),
+        name="asks",
+    )(here)
 
 
 def spread_kernel(arrived_ref, tails_ref, out_ref):
@@ -203,115 +232,71 @@
     core_ref,
     len_ref,
     here_ref,
-    k_ref,
-    v_ref,
-    sk_ref,
-    sv_ref,
+    asks_ref,
+    k0_ref,
+    k1_ref,
+    v0_ref,
+    v1_ref,
+    sk0_ref,
+    sk1_ref,
+    sv0_ref,
+    sv1_ref,
+    other_len_ref,
     bundle_ref,
     out_ref,
     w_ref,
-    k_buf,
-    v_buf,
-    sk_buf,
-    sv_buf,
-    len_buf,
     even_ref,
     odd_ref,
     sems,
 ):
-    step = pl.program_id(0)
-    steps = k_buf.shape[0]
+    step, steps = pl.program_id(0), pl.num_programs(0)
     total_heads = here_ref.shape[0]
     slots = here_ref.shape[1] - TAIL
-    length, wide = k_ref.shape
-    chips = total_heads * steps
-    own_suffix = sk_ref.shape[0]
-    spots = layout_of(length, chips, HEAD_SIZE, wide, own_suffix)
-    part = wide // steps
+    length, part = k0_ref.shape
     kv_heads = part // HEAD_SIZE
     heads = total_heads // kv_heads
-    parts = (
-        (k_ref, spots[0], length, k_buf),
-        (v_ref, spots[1], length, v_buf),
-        (sk_ref, spots[3], own_suffix, sk_buf),
-        (sv_ref, spots[4], own_suffix, sv_buf),
-    )
-
-    def copies(i, s):
-        ref, first, count, buf = parts[i]
-        columns = pl.ds(pl.multiple_of(s * part, part), part)
-        return (
-            pltpu.make_async_copy(
-                ref.at[:, columns], buf.at[s, pl.ds(0, count)], sems.at[s, 2 * i]
-            ),
-            pltpu.make_async_copy(
-                bundle_ref.at[pl.ds(first, count), columns],
-                buf.at[s, pl.ds(count, count)],
-                sems.at[s, 2 * i + 1],
-            ),
-        )
-
-    len_copy = pltpu.make_async_copy(
-        bundle_ref.at[pl.ds(spots[5], TAIL), :], len_buf, sems.at[0, 2 * len(parts)]
-    )
-
     w_copy = pltpu.make_async_copy(
-        bundle_ref.at[pl.ds(spots[2], w_ref.shape[0]), :], w_ref, sems.at[1, 2 * len(parts)]
+        bundle_ref.at[pl.ds(2 * length, w_ref.shape[0]), :], w_ref, sems.at[0]
     )
 
     @pl.when(step == 0)
     def _():
-        for s in range(steps):
-            for i in (0, 2, 3, 1):
-                for copy in copies(i, s):
-                    copy.start()
-            if s == 0:
-                len_copy.start()
         w_copy.start()
-        len_copy.wait()
-
-    def arrive(i):
-        for copy in copies(i, step):
-            copy.wait()
 
     cuts = [slice(j * HEAD_SIZE, (j + 1) * HEAD_SIZE) for j in range(kv_heads)]
-    ones = jnp.ones((2 * length, HEAD_SIZE), BF16)
+    ones = jnp.ones((length, HEAD_SIZE), BF16)
     held = (even_ref, odd_ref)
     units = [(j, j * heads + 2 * p) for j in range(kv_heads) for p in range(heads // 2)]
 
     def scores(unit):
         j, first = units[unit]
         query = jnp.concatenate([here_ref[first + i, :slots, :] for i in range(2)], axis=0)
-        value = matmul(query, k_buf[step, :, cuts[j]], 1, 1)
-        held[unit % 2][...] = value
-        return jnp.max(value, axis=1, keepdims=True)
-
-    arrive(0)
+        near = matmul(query, k0_ref[:, cuts[j]], 1, 1)
+        held[unit % 2][:, :length] = near
+        far = matmul(query, k1_ref[:, cuts[j]], 1, 1)
+        held[unit % 2][:, length:] = far
+        return jnp.max(jnp.maximum(near, far), axis=1, keepdims=True)
+
     peak = scores(0)
-    arrive(2)
-    arrive(3)
-    span = 2 * own_suffix
-    block = iota((1, span), 1) >> 7
-    others = len_buf[...].astype(F32)
+    others = other_len_ref[...].astype(F32)
     pick = lambda row: others[row : row + 1, :HEAD_SIZE].astype(jnp.int32)
     fixed = lambda row: jnp.full((1, HEAD_SIZE), len_ref[row], jnp.int32)
     lengths = jnp.concatenate([fixed(0), fixed(1), pick(0), pick(1)], axis=1)
     tails = []
     for j in range(kv_heads):
-        asks = jnp.concatenate([here_ref[j * heads + h, slots:, :] for h in range(heads)], axis=0)
+        asks = jnp.concatenate([asks_ref[j * heads + h] for h in range(heads)], axis=0)
+        both = lambda a, b: jnp.concatenate([a[:, cuts[j]], b[:, cuts[j]]], axis=0)
         tails.append(
-            suffix_part(
-                core_ref[0], lengths, asks, sk_buf[step, :, cuts[j]], sv_buf[step, :, cuts[j]]
-            )
+            suffix_part(core_ref[0], lengths, asks, both(sk0_ref, sk1_ref), both(sv0_ref, sv1_ref))
         )
-    arrive(1)
 
     lane = iota((2 * slots, HEAD_SIZE), 1)
     for unit, (j, start) in enumerate(units):
         peak_next = scores(unit + 1) if unit + 1 < len(units) else None
         shift = high_part(peak * FACTOR)
         weights = jnp.exp2(held[unit % 2][...] * (FACTOR * LOG2E) - shift * LOG2E).astype(BF16)
-        outs = matmul(weights, jnp.concatenate([v_buf[step, :, cuts[j]], ones], axis=1))
+        outs = matmul(weights[:, :length], jnp.concatenate([v0_ref[:, cuts[j]], ones], axis=1))
+        outs += matmul(weights[:, length:], jnp.concatenate([v1_ref[:, cuts[j]], ones], axis=1))
         total = outs[:, HEAD_SIZE:]
         total_high = high_part(total)
         numbers = jnp.where(
@@ -333,32 +318,46 @@
         w_copy.wait()
 
 
-def attend(core, lengths, here, keys, values, skeys, svalues, bundle):
+def attend(core, lengths, here, asks, keys, values, skeys, svalues, bundle):
     chips, height, _ = here.shape
     steps = 2
     heads = chips // steps
     length, wide = keys.shape
     part = wide // steps
     slots, own_suffix = height - TAIL, skeys.shape[0]
+    spots = layout_of(length, chips, HEAD_SIZE, wide, own_suffix)
     chunk = pl.BlockSpec((heads, height, HEAD_SIZE), lambda j: (j, 0, 0))
+    tail = pl.BlockSpec((heads, TAIL, HEAD_SIZE), lambda j: (j, 0, 0))
+    block = lambda rows, first: pl.BlockSpec((rows, part), lambda j: (first // rows, j))
+    w_rows = chips * HEAD_SIZE // 2
     return pl.pallas_call(
         attend_kernel,
         grid=(steps,),
-        in_specs=[SMEM, SMEM, chunk] + [HBM] * 5,
-        out_specs=(chunk, whole_spec((chips * HEAD_SIZE // 2, wide))),
+        in_specs=[
+            SMEM,
+            SMEM,
+            chunk,
+            tail,
+            block(length, 0),
+            block(length, spots[0]),
+            block(length, 0),
+            block(length, spots[1]),
+            block(own_suffix, 0),
+            block(own_suffix, spots[3]),
+            block(own_suffix, 0),
+            block(own_suffix, spots[4]),
+            pl.BlockSpec((TAIL, HEAD_SIZE), lambda j: (spots[5] // TAIL, 0)),
+            HBM,
+        ],
+        out_specs=(chunk, whole_spec((w_rows, wide))),
         out_shape=(
             jax.ShapeDtypeStruct(here.shape, BF16),
-            jax.ShapeDtypeStruct((chips * HEAD_SIZE // 2, wide), BF16),
+            jax.ShapeDtypeStruct((w_rows, wide), BF16),
         ),
         scratch_shapes=[
-            pltpu.VMEM((steps, 2 * length, part), BF16),
-            pltpu.VMEM((steps, 2 * length, part), BF16),
-            pltpu.VMEM((steps, 2 * own_suffix, part), BF16),
-            pltpu.VMEM((steps, 2 * own_suffix, part), BF16),
-            pltpu.VMEM((TAIL, wide), BF16),
             pltpu.VMEM((2 * slots, 2 * length), F32),
             pltpu.VMEM((2 * slots, 2 * length), F32),
-            pltpu.SemaphoreType.DMA((steps, 9)),
+            pltpu.SemaphoreType.DMA((1,)),
         ],
         compiler_params=pltpu.CompilerParams(vmem_limit_bytes=36 * 1024 * 1024),
         cost_estimate=pl.CostEstimate(
@@ -367,7 +366,22 @@
             transcendentals=2 * chips * height * length,
         ),
         name="attend",
-    )(core, lengths, here, keys, values, skeys, svalues, bundle)
+    )(
+        core,
+        lengths,
+        here,
+        asks,
+        keys,
+        bundle,
+        values,
+        bundle,
+        skeys,
+        bundle,
+        svalues,
+        bundle,
+        bundle,
+        bundle,
+    )
 
 
 def merge_kernel(own_ref, sent_ref):
@@ -504,26 +518,18 @@
     skeys = row_suffix_keys.reshape(-1, row_suffix_keys.shape[2])
     svalues = row_suffix_values.reshape(-1, row_suffix_values.shape[2])
 
-    packed, place, tails, bundle = pack(
-        core,
-        suffix_lengths,
-        row_prompt.reshape(1, row_grp),
-        queries,
-        keys,
-        values,
-        skeys,
-        svalues,
-        w_out,
-        slots,
-        chips,
-    )
+    packed, place, tails = pack(row_prompt.reshape(1, row_grp), queries, slots, chips)
+    arrived = lax.all_to_all(packed, "grp", split_axis=0, concat_axis=0, tiled=True)
+
+    _, late_lengths = lax.optimization_barrier((arrived, suffix_lengths))
+    bundle = bundled(core, late_lengths, keys, values, skeys, svalues, w_out)
     bundle = lax.ppermute(bundle, "core", SWAP)
-    arrived = lax.all_to_all(packed, "grp", split_axis=0, concat_axis=0, tiled=True)
-
     here = lax.all_to_all(
         spread(arrived, tails, chips), PLANE, split_axis=0, concat_axis=0, tiled=True
     )
-    parts, w_other = attend(core, suffix_lengths, here, keys, values, skeys, svalues, bundle)
+    parts, w_other = attend(
+        core, suffix_lengths, here, asks_of(here), keys, values, skeys, svalues, bundle
+    )
     own = lax.all_to_all(parts, PLANE, split_axis=0, concat_axis=0, tiled=True)
 
     sent = merge(own, groups)

time: 116 us -> 122 us (1.052)
  blocking collectives: 85.6 us -> 66.1 us
  waiting for transfers between devices: 0.01 us -> 11.5 us
  starting transfers between devices: 8.77 us -> 19.7 us
  local copies, waits for them, and re-layouts: 3.06 us -> 5.24 us
    all_to_all x1 -> x0, blocking collectives: 21 us -> none  [body(): lax.all_to_all(packed, 'grp', split_axis=0, concat_axis=0, tiled=True)]
    all_to_all x0 -> x1, starting transfers between devices: none -> 15.7 us  [body(): lax.all_to_all(packed, 'grp', split_axis=0, concat_axis=0, tiled=True)]
    all_to_all x0 -> x1, waiting for transfers between devices: none -> 11.5 us  [body(): lax.all_to_all(packed, 'grp', split_axis=0, concat_axis=0, tiled=True)]
    ppermute x1, starting transfers between devices: 8.77 us -> 3.95 us  [body(): bundle = lax.ppermute(bundle, 'core', SWAP)]
    unnamed x20 -> x28, local copies, waits for them, and re-layouts: 3.06 us -> 5.24 us
    all_to_all x1, blocking collectives: 16.9 us -> 18.5 us  [body(): lax.all_to_all(spread(arrived, tails, chips), PLANE, split_axis=0, concat...]
    pallas_call x2 -> x4, Pallas kernels: 13.7 us -> 14.4 us  [the longest x1 7.62 us: attend(): pl.pallas_call(attend_kernel, grid=(steps,), in_specs=[SMEM, SMEM, chunk,...]
  transfers between devices with their start and end apart: 1 -> 2, of which waited for: 0 -> 1; matrix products, arithmetic and copies ran while one was open for 0% -> 0% of each run, Pallas kernels for 0% -> 1%
where the time goes in v3:
time: 122 us; the launch traced here: 121 us
  blocking collectives  66.1 us (54%)
  starting transfers between devices  19.7 us (16%)
  Pallas kernels  17.8 us (15%)
  waiting for transfers between devices  11.5 us (9%)
  local copies, waits for them, and re-layouts  5.24 us (4%)
    all_to_all x1, blocking collectives, body(): lax.all_to_all(spread(arrived, tails, chips), PLANE, split_axis=0, concat...  18.5 us
    all_to_all x1, starting transfers between devices, body(): lax.all_to_all(packed, 'grp', split_axis=0, concat_axis=0, tiled=True)  15.7 us
    all_to_all x1, blocking collectives, body(): back = lax.all_to_all(sent, 'grp', split_axis=0, concat_axis=0, tiled=True)  14.9 us
    all_to_all x1, blocking collectives, body(): own = lax.all_to_all(parts, PLANE, split_axis=0, concat_axis=0, tiled=True)  13.8 us
    all_to_all x1, blocking collectives, body(): lax.all_to_all(shares, PLANE, split_axis=0, concat_axis=0, tiled=True)  13.3 us
    all_to_all x1, waiting for transfers between devices, body(): lax.all_to_all(packed, 'grp', split_axis=0, concat_axis=0, tiled=True)  11.5 us
    pallas_call x1, Pallas kernels, attend(): pl.pallas_call(attend_kernel, grid=(steps,), in_specs=[SMEM, SMEM, chunk,...  7.62 us
    all_gather x1, blocking collectives, body(): lax.all_gather(finish(place, back, own), 'core', axis=0, tiled=False)  5.53 us
  transfers between devices with their start and end apart: 2, of which 1 were waited for; matrix products, arithmetic and copies ran while one was open for 0% of the time, Pallas kernels for 1%

profile of v3, /device:TPU:1, one launch (start us, length us, event | category | flops | bytes accessed | tf_op | source)
XLA Modules:
  0.0 121.1 jit_solution(7819920758307718229)
XLA Ops:
  0.0 0.0 copy-start.11
  0.0 0.7 copy-done.11
  0.7 0.0 copy-start.13
  0.7 0.7 copy-done.13
  1.4 0.9 pack.1
  2.3 0.0 copy-start.10
  2.3 0.6 copy-done.10
  2.9 15.7 %all-to-all-start = ((bf16[16,8,128]{2,1,0:T(8,128)(2,1)}), bf16[16,8,128]{2,1,0:T(8,128)(2,1)S(1)}, u32[]{:S(2)}, u32[]{:S(2)}) async-start(bf16[16,8,128]{2,1,0:T(8,128)(2,1)} %bitcast.2), calls=%async_computation | async-start | bytes 65536 | tf_op jit(solution)/shard_map/all_to_all | solution.py:522
  18.7 11.5 %all-to-all-done = bf16[16,8,128]{2,1,0:T(8,128)(2,1)S(1)} async-done(((bf16[16,8,128]{2,1,0:T(8,128)(2,1)}), bf16[16,8,128]{2,1,0:T(8,128)(2,1)S(1)}, u32[]{:S(2)}, u32[]{:S(2)}) %all-to-all-start) | async-done | bytes 32800 | tf_op jit(solution)/shard_map/all_to_all | solution.py:522
  30.1 4.2 %bundle.1 = bf16[3600,512]{1,0:T(8,128)(2,1)} custom-call(s32[1]{0:T(128)} %bitcast.core_ref, s32[2]{0:T(128)} %len_ref.2, bf16[1024,512]{1,0:T(8,128)(2,1)} %bitcast.9, bf16[1024,512]{1,0:T(8,128)(2,1)} %bitcast.11, bf16[256,512]{1,0:T(8,128)(2,1)} %bitcast.13, bf16[256,512]{1,0:T(8,128)(2,1)} %bitcast.15, bf16[128,8192]{1,0:T(8,128)(2,1)} %w0_ref.1), custom_call_target="tpu_custom_call" | custom-call | tf_op jit(solution)/shard_map/bundle/pallas_call | solution.py:153
  34.3 4.0 %collective-permute-start = (bf16[3600,512]{1,0:T(8,128)(2,1)}, bf16[3600,512]{1,0:T(8,128)(2,1)}, u32[]{:S(2)}, u32[]{:S(2)}) collective-permute-start(bf16[3600,512]{1,0:T(8,128)(2,1)} %bundle.1), channel_id=1, source_target_pairs={{0,1},{1,0},{2,3},{3,2},{4,5},{5,4},{6,7},{7,6},{8,9},{9,8},{10,11... | collective-permute-start | bytes 11059208 | tf_op jit(solution)/shard_map/ppermute | solution.py:526
  38.3 0.1 spread.1
  38.4 18.5 %all_to_all.31.here_ref = bf16[16,144,128]{2,1,0:T(8,128)(2,1)} all-to-all(bf16[16,144,128]{2,1,0:T(8,128)(2,1)S(1)} %spread.1), channel_id=1, replica_groups=mesh['grp'=16,'x'=4,'y'=4,'core'=2] {'x','y'}, dimensions={0} | all-to-all | bytes 1179648 | tf_op jit(solution)/shard_map/all_to_all | solution.py:527
  56.9 0.0 copy-start.2
  56.9 0.0 copy-start.3
  56.9 0.0 copy-start.4
  56.9 0.0 copy-start.5
  56.9 0.0 copy-start.6
  56.9 0.0 copy-start.12
  56.9 1.6 %asks.1.asks_ref = bf16[16,16,128]{2,1,0:T(8,128)(2,1)} custom-call(bf16[16,144,128]{2,1,0:T(8,128)(2,1)} %all_to_all.31.here_ref), custom_call_target="tpu_custom_call" | custom-call | flops 20000000000 | bytes 1048576 | tf_op jit(solution)/shard_map/asks/pallas_call | solution.py:174
  58.6 0.0 collective-permute-done.k1_ref.v1_ref.sk1_ref.sv1_ref.other_len_ref.bundle_ref
  58.6 0.0 copy-done.2
  58.6 0.0 copy-done.3
  58.6 0.1 copy-done.4
  58.6 0.1 copy-done.5
  58.7 0.1 copy-done.6
  58.8 0.0 copy-done.12
  58.8 0.0 copy-start.9
  58.8 0.8 copy-done.9
  59.6 7.6 %attend.1 = (bf16[16,144,128]{2,1,0:T(8,128)(2,1)S(1)}, bf16[1024,512]{1,0:T(8,128)(2,1)S(1)}) custom-call(s32[1]{0:T(128)} %bitcast.core_ref, s32[2]{0:T(128)S(1)} %copy-done.12, bf16[16,144,128]{2,1,0:T(8,128)(2,1)S(1)} %copy-done.4, bf16[16,16,128]{2,1,0:T(8,128)(2,1)S(1)} %copy-done.9, bf16[1024,512]{1,0:T(8,128)(2,1)S(1)} %bitcast.10, ...), custom_call_target="tpu_custom_call" | custom-call | flops 2415919104 | bytes 5242880 | tf_op jit(solution)/shard_map/attend/pallas_call | solution.py:333
  67.2 0.0 copy-start.7
  67.3 1.0 copy-done.7
  68.2 0.0 copy-start
  68.2 13.8 %all_to_all.32.own_ref.tails_ref = bf16[16,144,128]{2,1,0:T(8,128)(2,1)S(1)} all-to-all(bf16[16,144,128]{2,1,0:T(8,128)(2,1)S(1)} %get-tuple-element.15), channel_id=1, replica_groups=mesh['grp'=16,'x'=4,'y'=4,'core'=2] {'x','y'}, dimensions={0} | all-to-all | bytes 1179648 | tf_op jit(solution)/shard_map/all_to_all | solution.py:533
  82.0 0.0 copy-start.1
  82.0 0.5 merge.1
  82.6 14.9 %all_to_all.33.back_ref = bf16[16,16,128]{2,1,0:T(8,128)(2,1)} all-to-all(bf16[16,16,128]{2,1,0:T(8,128)(2,1)S(1)} %merge.1), channel_id=1, replica_groups=mesh['grp'=16,'x'=4,'y'=4,'core'=2] {'grp'}, dimensions={0} | all-to-all | bytes 131072 | tf_op jit(solution)/shard_map/all_to_all | solution.py:536
  97.5 0.0 copy-done.1
  97.5 2.0 %finish.1 = bf16[64,128]{1,0:T(8,128)(2,1)} custom-call(bf16[128,64]{1,0:T(8,128)(2,1)} %copy-done.10, bf16[16,16,128]{2,1,0:T(8,128)(2,1)} %all_to_all.33.back_ref, bf16[16,144,128]{2,1,0:T(8,128)(2,1)} %copy-done.1), custom_call_target="tpu_custom_call" | custom-call | tf_op jit(solution)/shard_map/finish/pallas_call | solution.py:454
  99.5 5.5 %all-gather = bf16[128,128]{1,0:T(8,128)(2,1)S(1)} all-gather(bf16[64,128]{1,0:T(8,128)(2,1)} %finish.1), channel_id=2, replica_groups=mesh['grp'=16,'x'=4,'y'=4,'core'=2] {'core'}, dimensions={0}, use_global_device_ids=true | all-gather | bytes 49152 | tf_op jit(solution)/shard_map/all_gather | solution.py:537
  105.0 0.0 copy-done
  105.0 0.0 copy-start.8
  105.0 1.2 %copy-done.8 = bf16[1024,512]{1,0:T(8,128)(2,1)S(1)} copy-done((bf16[1024,512]{1,0:T(8,128)(2,1)S(1)}, bf16[1024,512]{1,0:T(8,128)(2,1)}, u32[]{:S(2)}) %copy-start.8) | copy-done | bytes 1048600
  106.2 0.8 project.1
  107.1 13.3 %all_to_all.34 = bf16[16,64,256]{2,1,0:T(8,128)(2,1)S(1)} all-to-all(bf16[16,64,256]{2,1,0:T(8,128)(2,1)S(1)} %project.1), channel_id=1, replica_groups=mesh['grp'=16,'x'=4,'y'=4,'core'=2] {'x','y'}, dimensions={0} | all-to-all | bytes 1048576 | tf_op jit(solution)/shard_map/all_to_all | solution.py:539
  120.4 0.7 reduce_sum.12
Async XLA Ops:
  0.0 0.7 copy-start.11
  0.7 0.7 copy-start.13
  2.3 0.6 copy-start.10
  2.9 27.2 %all-to-all-start = ((bf16[16,8,128]{2,1,0:T(8,128)(2,1)}), bf16[16,8,128]{2,1,0:T(8,128)(2,1)S(1)}, u32[]{:S(2)}, u32[]{:S(2)}) async-start(bf16[16,8,128]{2,1,0:T(8,128)(2,1)} %bitcast.2), calls=%async_computation | async-start | bytes 65536 | tf_op jit(solution)/shard_map/all_to_all | solution.py:522
  34.3 24.2 %collective-permute-start = (bf16[3600,512]{1,0:T(8,128)(2,1)}, bf16[3600,512]{1,0:T(8,128)(2,1)}, u32[]{:S(2)}, u32[]{:S(2)}) collective-permute-start(bf16[3600,512]{1,0:T(8,128)(2,1)} %bundle.1), channel_id=1, source_target_pairs={{0,1},{1,0},{2,3},{3,2},{4,5},{5,4},{6,7},{7,6},{8,9},{9,8},{10,11... | collective-permute-start | bytes 11059208 | tf_op jit(solution)/shard_map/ppermute | solution.py:526
  56.9 1.7 %copy-start.2 = (bf16[1,1024,512]{2,1,0:T(8,128)(2,1)S(1)}, bf16[1,1024,512]{2,1,0:T(8,128)(2,1)}, u32[]{:S(2)}) copy-start(bf16[1,1024,512]{2,1,0:T(8,128)(2,1)} %param.10) | copy-start | bytes 3145732
  56.9 1.7 %copy-start.3 = (bf16[1,1024,512]{2,1,0:T(8,128)(2,1)S(1)}, bf16[1,1024,512]{2,1,0:T(8,128)(2,1)}, u32[]{:S(2)}) copy-start(bf16[1,1024,512]{2,1,0:T(8,128)(2,1)} %param.11) | copy-start | bytes 3145732
  56.9 1.7 %copy-start.4 = (bf16[16,144,128]{2,1,0:T(8,128)(2,1)S(1)}, bf16[16,144,128]{2,1,0:T(8,128)(2,1)}, u32[]{:S(2)}) copy-start(bf16[16,144,128]{2,1,0:T(8,128)(2,1)} %all_to_all.31.here_ref) | copy-start | bytes 1769476
  56.9 1.8 %copy-start.5 = (bf16[2,128,512]{2,1,0:T(8,128)(2,1)S(1)}, bf16[2,128,512]{2,1,0:T(8,128)(2,1)}, u32[]{:S(2)}) copy-start(bf16[2,128,512]{2,1,0:T(8,128)(2,1)} %param.12) | copy-start | bytes 786436
  56.9 1.9 %copy-start.6 = (bf16[2,128,512]{2,1,0:T(8,128)(2,1)S(1)}, bf16[2,128,512]{2,1,0:T(8,128)(2,1)}, u32[]{:S(2)}) copy-start(bf16[2,128,512]{2,1,0:T(8,128)(2,1)} %param.13) | copy-start | bytes 786436
  56.9 1.8 %copy-start.12 = (s32[2]{0:T(128)S(1)}, s32[2]{0:T(128)}, u32[]{:S(2)}) copy-start(s32[2]{0:T(128)} %len_ref.2) | copy-start | bytes 28
  58.8 0.8 copy-start.9
  67.2 1.0 copy-start.7
  68.2 36.8 %copy-start = (bf16[128,8192]{1,0:T(8,128)(2,1)S(1)}, bf16[128,8192]{1,0:T(8,128)(2,1)}, u32[]{:S(2)}) copy-start(bf16[128,8192]{1,0:T(8,128)(2,1)} %w0_ref.1) | copy-start | bytes 6291460
  82.0 15.4 %copy-start.1 = (bf16[16,144,128]{2,1,0:T(8,128)(2,1)}, bf16[16,144,128]{2,1,0:T(8,128)(2,1)S(1)}, u32[]{:S(2)}) copy-start(bf16[16,144,128]{2,1,0:T(8,128)(2,1)S(1)} %all_to_all.32.own_ref.tails_ref) | copy-start | bytes 1769476
  105.0 1.2 %copy-start.8 = (bf16[1024,512]{1,0:T(8,128)(2,1)S(1)}, bf16[1024,512]{1,0:T(8,128)(2,1)}, u32[]{:S(2)}) copy-start(bf16[1024,512]{1,0:T(8,128)(2,1)} %copy-done.7) | copy-start | bytes 3145732

commit v4 on v2

--- a/solution.py
+++ b/solution.py
@@ -19,6 +19,7 @@
 LOG2E = 1.0 / math.log(2.0)
 BIG = 28 * 1024 * 1024
 MOST = 58 * 1024 * 1024
+ROOMY = 24 * 1024
 F32, BF16 = jnp.float32, jnp.bfloat16
 
 
@@ -210,6 +211,7 @@
     bundle_ref,
     out_ref,
     w_ref,
+    w_buf,
     k_buf,
     v_buf,
     sk_buf,
@@ -255,9 +257,13 @@
         bundle_ref.at[pl.ds(spots[5], TAIL), :], len_buf, sems.at[0, 2 * len(parts)]
     )
 
-    w_copy = pltpu.make_async_copy(
-        bundle_ref.at[pl.ds(spots[2], w_ref.shape[0]), :], w_ref, sems.at[1, 2 * len(parts)]
-    )
+    w_in = pltpu.make_async_copy(
+        bundle_ref.at[pl.ds(spots[2], w_buf.shape[0]), :], w_buf, sems.at[1, 2 * len(parts)]
+    )
+    w_out = pltpu.make_async_copy(
+        w_buf, w_ref.at[pl.ds(0, w_buf.shape[0]), :], sems.at[0, 2 * len(parts) + 1]
+    )
+
 
     @pl.when(step == 0)
     def _():
@@ -267,8 +273,13 @@
                     copy.start()
             if s == 0:
                 len_copy.start()
-        w_copy.start()
+        w_in.start()
         len_copy.wait()
+
+    @pl.when(step == steps - 1)
+    def _():
+        w_in.wait()
+        w_out.start()
 
     def arrive(i):
         for copy in copies(i, step):
@@ -330,7 +341,7 @@
 
     @pl.when(step == steps - 1)
     def _():
-        w_copy.wait()
+        w_out.wait()
 
 
 def attend(core, lengths, here, keys, values, skeys, svalues, bundle):
@@ -345,12 +356,13 @@
         attend_kernel,
         grid=(steps,),
         in_specs=[SMEM, SMEM, chunk] + [HBM] * 5,
-        out_specs=(chunk, whole_spec((chips * HEAD_SIZE // 2, wide))),
+        out_specs=(chunk, HBM),
         out_shape=(
             jax.ShapeDtypeStruct(here.shape, BF16),
-            jax.ShapeDtypeStruct((chips * HEAD_SIZE // 2, wide), BF16),
+            jax.ShapeDtypeStruct((ROOMY, wide), BF16),
         ),
         scratch_shapes=[
+            pltpu.VMEM((chips * HEAD_SIZE // 2, wide), BF16),
             pltpu.VMEM((steps, 2 * length, part), BF16),
             pltpu.VMEM((steps, 2 * length, part), BF16),
             pltpu.VMEM((steps, 2 * own_suffix, part), BF16),
@@ -358,9 +370,9 @@
             pltpu.VMEM((TAIL, wide), BF16),
             pltpu.VMEM((2 * slots, 2 * length), F32),
             pltpu.VMEM((2 * slots, 2 * length), F32),
-            pltpu.SemaphoreType.DMA((steps, 9)),
+            pltpu.SemaphoreType.DMA((steps, 10)),
         ],
-        compiler_params=pltpu.CompilerParams(vmem_limit_bytes=36 * 1024 * 1024),
+        compiler_params=pltpu.CompilerParams(vmem_limit_bytes=40 * 1024 * 1024),
         cost_estimate=pl.CostEstimate(
             flops=8 * chips * height * length * HEAD_SIZE,
             bytes_accessed=10 * length * wide,

time: 116 us -> 114 us (0.983)
  local copies, waits for them, and re-layouts: 3.06 us -> 0.87 us
    unnamed x20 -> x16, local copies, waits for them, and re-layouts: 3.06 us -> 0.87 us
where the time goes in v4:
time: 114 us
  blocking collectives  85.5 us (75%)
  Pallas kernels  18 us (16%)
  starting transfers between devices  8.77 us (8%)
    all_to_all x1, blocking collectives, body(): lax.all_to_all(packed, 'grp', split_axis=0, concat_axis=0, tiled=True)  21 us
    all_to_all x1, blocking collectives, body(): lax.all_to_all(spread(arrived, tails, chips), PLANE, split_axis=0, concat...  16.9 us
    all_to_all x1, blocking collectives, body(): back = lax.all_to_all(sent, 'grp', split_axis=0, concat_axis=0, tiled=True)  14.9 us
    all_to_all x1, blocking collectives, body(): lax.all_to_all(shares, PLANE, split_axis=0, concat_axis=0, tiled=True)  13.3 us
    all_to_all x1, blocking collectives, body(): own = lax.all_to_all(parts, PLANE, split_axis=0, concat_axis=0, tiled=True)  12.7 us
    ppermute x1, starting transfers between devices, body(): bundle = lax.ppermute(bundle, 'core', SWAP)  8.77 us
    pallas_call x1, Pallas kernels, attend(): pl.pallas_call(attend_kernel, grid=(steps,), in_specs=[SMEM, SMEM, chunk]...  8.46 us
    all_gather x1, blocking collectives, body(): lax.all_gather(finish(place, back, own), 'core', axis=0, tiled=False)  6.67 us
  transfers between devices with their start and end apart: 1, of which 0 were waited for; matrix products, arithmetic and copies ran while one was open for 0% of the time, Pallas kernels for 0%

profile of v4, /device:TPU:1, one launch (start us, length us, event | category | flops | bytes accessed | tf_op | source)
XLA Modules:
  0.0 114.0 jit_solution(10795502802609620065)
XLA Ops:
  0.0 0.0 copy-start.7
  0.0 0.0 copy-start.4
  0.0 0.0 copy-start.2
  0.0 0.0 copy-start.3
  0.0 0.0 copy-start.5
  0.0 5.2 %pack.1 = (bf16[128,128]{1,0:T(8,128)(2,1)}, bf16[128,64]{1,0:T(8,128)(2,1)}, bf16[256,128]{1,0:T(8,128)(2,1)}, bf16[3600,512]{1,0:T(8,128)(2,1)}) custom-call(s32[1]{0:T(128)} %bitcast.core_ref, s32[2]{0:T(128)} %len_ref.3, s32[1,64]{1,0:T(1,128)} %bitcast.20, bf16[64,128]{1,0:T(8,128)(2,1)} %query_ref.1, bf16[1024,512]{1,0:T(8,128)(2,1)} %bitcast.9, ...), custom_call_target="tpu_custom_call" | custom-call | tf_op jit(solution)/shard_map/pack/pallas_call | solution.py:141
  5.3 8.8 %collective-permute-start = (bf16[3600,512]{1,0:T(8,128)(2,1)}, bf16[3600,512]{1,0:T(8,128)(2,1)S(1)}, u32[]{:S(2)}, u32[]{:S(2)}) collective-permute-start(bf16[3600,512]{1,0:T(8,128)(2,1)} %get-tuple-element.14), channel_id=1, source_target_pairs={{0,1},{1,0},{2,3},{3,2},{4,5},{5,4},{6,7},{7,6},{8,9},{9,8},{10,11... | collective-permute-start | bytes 11059208 | tf_op jit(solution)/shard_map/ppermute | solution.py:532
  14.0 21.0 %all_to_all.31 = bf16[16,8,128]{2,1,0:T(8,128)(2,1)S(1)} all-to-all(bf16[16,8,128]{2,1,0:T(8,128)(2,1)} %bitcast.19), channel_id=1, replica_groups=mesh['grp'=16,'x'=4,'y'=4,'core'=2] {'grp'}, dimensions={0} | all-to-all | bytes 65536 | tf_op jit(solution)/shard_map/all_to_all | solution.py:533
  35.1 0.0 copy-start.6
  35.1 0.8 copy-done.6
  35.9 0.1 spread.1
  36.0 16.9 %all_to_all.32.here_ref = bf16[16,144,128]{2,1,0:T(8,128)(2,1)S(1)} all-to-all(bf16[16,144,128]{2,1,0:T(8,128)(2,1)S(1)} %spread.1), channel_id=1, replica_groups=mesh['grp'=16,'x'=4,'y'=4,'core'=2] {'x','y'}, dimensions={0} | all-to-all | bytes 1179648 | tf_op jit(solution)/shard_map/all_to_all | solution.py:535
  52.9 0.0 copy-start
  52.9 0.0 collective-permute-done.bundle_ref
  52.9 0.0 copy-done.7
  52.9 0.0 copy-done.4
  52.9 0.0 copy-done.2
  52.9 0.0 copy-done.3
  52.9 0.0 copy-done.5
  52.9 8.5 %attend.1 = (bf16[16,144,128]{2,1,0:T(8,128)(2,1)S(1)}, bf16[24576,512]{1,0:T(8,128)(2,1)}) custom-call(s32[1]{0:T(128)} %bitcast.core_ref, s32[2]{0:T(128)S(1)} %copy-done.7, bf16[16,144,128]{2,1,0:T(8,128)(2,1)S(1)} %all_to_all.32.here_ref, bf16[1024,512]{1,0:T(8,128)(2,1)S(1)} %bitcast.10, bf16[1024,512]{1,0:T(8,128)(2,1)S(1)} %bitcast.12, ...), custom_call_target="tpu_custom_call" | custom-call | flops 2415919104 | bytes 5242880 | tf_op jit(solution)/shard_map/attend/pallas_call | solution.py:355
  61.4 12.7 %all_to_all.33.own_ref.tails_ref = bf16[16,144,128]{2,1,0:T(8,128)(2,1)S(1)} all-to-all(bf16[16,144,128]{2,1,0:T(8,128)(2,1)S(1)} %get-tuple-element.15), channel_id=1, replica_groups=mesh['grp'=16,'x'=4,'y'=4,'core'=2] {'x','y'}, dimensions={0} | all-to-all | bytes 1179648 | tf_op jit(solution)/shard_map/all_to_all | solution.py:539
  74.1 0.0 copy-start.1
  74.1 0.5 merge.1
  74.6 14.9 %all_to_all.34.back_ref = bf16[16,16,128]{2,1,0:T(8,128)(2,1)} all-to-all(bf16[16,16,128]{2,1,0:T(8,128)(2,1)S(1)} %merge.1), channel_id=1, replica_groups=mesh['grp'=16,'x'=4,'y'=4,'core'=2] {'grp'}, dimensions={0} | all-to-all | bytes 131072 | tf_op jit(solution)/shard_map/all_to_all | solution.py:542
  89.5 0.0 copy-done.1
  89.5 2.0 %finish.1 = bf16[64,128]{1,0:T(8,128)(2,1)} custom-call(bf16[128,64]{1,0:T(8,128)(2,1)} %get-tuple-element.11.place_ref, bf16[16,16,128]{2,1,0:T(8,128)(2,1)} %all_to_all.34.back_ref, bf16[16,144,128]{2,1,0:T(8,128)(2,1)} %copy-done.1), custom_call_target="tpu_custom_call" | custom-call | tf_op jit(solution)/shard_map/finish/pallas_call | solution.py:452
  91.5 6.7 %all-gather = bf16[128,128]{1,0:T(8,128)(2,1)S(1)} all-gather(bf16[64,128]{1,0:T(8,128)(2,1)} %finish.1), channel_id=2, replica_groups=mesh['grp'=16,'x'=4,'y'=4,'core'=2] {'core'}, dimensions={0}, use_global_device_ids=true | all-gather | bytes 49152 | tf_op jit(solution)/shard_map/all_gather | solution.py:543
  98.2 0.0 copy-done
  98.2 1.8 %project.1 = bf16[16,64,256]{2,1,0:T(8,128)(2,1)S(1)} custom-call(s32[1]{0:T(128)} %bitcast.core_ref, bf16[2,64,128]{2,1,0:T(8,128)(2,1)S(1)} %bitcast.17, bf16[128,8192]{1,0:T(8,128)(2,1)S(1)} %copy-done, bf16[24576,512]{1,0:T(8,128)(2,1)} %get-tuple-element.16.w1_ref), custom_call_target="tpu_custom_call" | custom-call | tf_op jit(solution)/shard_map/project/pallas_call | solution.py:484
  100.0 13.3 %all_to_all.35 = bf16[16,64,256]{2,1,0:T(8,128)(2,1)S(1)} all-to-all(bf16[16,64,256]{2,1,0:T(8,128)(2,1)S(1)} %project.1), channel_id=1, replica_groups=mesh['grp'=16,'x'=4,'y'=4,'core'=2] {'x','y'}, dimensions={0} | all-to-all | bytes 1048576 | tf_op jit(solution)/shard_map/all_to_all | solution.py:545
  113.3 0.7 reduce_sum.12
Async XLA Ops:
  0.0 52.9 %copy-start.7 = (s32[2]{0:T(128)S(1)}, s32[2]{0:T(128)}, u32[]{:S(2)}) copy-start(s32[2]{0:T(128)} %len_ref.3) | copy-start | bytes 28
  0.0 52.9 %copy-start.4 = (bf16[2,128,512]{2,1,0:T(8,128)(2,1)S(1)}, bf16[2,128,512]{2,1,0:T(8,128)(2,1)}, u32[]{:S(2)}) copy-start(bf16[2,128,512]{2,1,0:T(8,128)(2,1)} %param.12) | copy-start | bytes 786436
  0.0 52.9 %copy-start.2 = (bf16[1,1024,512]{2,1,0:T(8,128)(2,1)S(1)}, bf16[1,1024,512]{2,1,0:T(8,128)(2,1)}, u32[]{:S(2)}) copy-start(bf16[1,1024,512]{2,1,0:T(8,128)(2,1)} %param.10) | copy-start | bytes 3145732
  0.0 52.9 %copy-start.3 = (bf16[1,1024,512]{2,1,0:T(8,128)(2,1)S(1)}, bf16[1,1024,512]{2,1,0:T(8,128)(2,1)}, u32[]{:S(2)}) copy-start(bf16[1,1024,512]{2,1,0:T(8,128)(2,1)} %param.11) | copy-start | bytes 3145732
  0.0 52.9 %copy-start.5 = (bf16[2,128,512]{2,1,0:T(8,128)(2,1)S(1)}, bf16[2,128,512]{2,1,0:T(8,128)(2,1)}, u32[]{:S(2)}) copy-start(bf16[2,128,512]{2,1,0:T(8,128)(2,1)} %param.13) | copy-start | bytes 786436
  5.3 47.6 %collective-permute-start = (bf16[3600,512]{1,0:T(8,128)(2,1)}, bf16[3600,512]{1,0:T(8,128)(2,1)S(1)}, u32[]{:S(2)}, u32[]{:S(2)}) collective-permute-start(bf16[3600,512]{1,0:T(8,128)(2,1)} %get-tuple-element.14), channel_id=1, source_target_pairs={{0,1},{1,0},{2,3},{3,2},{4,5},{5,4},{6,7},{7,6},{8,9},{9,8},{10,11... | collective-permute-start | bytes 11059208 | tf_op jit(solution)/shard_map/ppermute | solution.py:532
  35.1 0.8 copy-start.6
  52.9 45.3 %copy-start = (bf16[128,8192]{1,0:T(8,128)(2,1)S(1)}, bf16[128,8192]{1,0:T(8,128)(2,1)}, u32[]{:S(2)}) copy-start(bf16[128,8192]{1,0:T(8,128)(2,1)} %w0_ref.1) | copy-start | bytes 6291460
  74.1 15.4 %copy-start.1 = (bf16[16,144,128]{2,1,0:T(8,128)(2,1)}, bf16[16,144,128]{2,1,0:T(8,128)(2,1)S(1)}, u32[]{:S(2)}) copy-start(bf16[16,144,128]{2,1,0:T(8,128)(2,1)S(1)} %all_to_all.33.own_ref.tails_ref) | copy-start | bytes 1769476
